TPU v7x, 512 devices: a whole 4x4x16 slice. The times are simulated.
512 devices in a mesh: segment: 16 (over y, x_hi, core), dp: 32 (over z, x_lo).
Axes of the slice: x: 4 (x_hi: 2, x_lo: 2; x = x_hi * 2 + x_lo), y: 4, z: 16, core: 2. Of those that a mesh axis runs over, the one named last changes fastest.
Arguments:
- hidden_in: bfloat16 [8, 512, 9216], P(None, 'dp', 'segment'), may hold values from -6 to 6
- cotangent: bfloat16 [8, 512, 9216], P(None, 'dp', 'segment'), may hold values from -0.25 to 0.25
- stored_bases: bfloat16 [16, 8, 512, 9216], P('segment', None, 'dp'), may hold values from -6 to 6
- sample_ids: int32 [32, 8], P('dp'), may hold values from 0 to 7, each once within a row
- block_exps: int32 [16, 8, 512, 72], P('segment', None, 'dp'), may hold values from -9 to -4
- ln_gains: bfloat16 [16, 9216], P('segment'), may hold values from 0.099609375 to 1.8984375
- w_down: bfloat16 [16, 9216, 16], P('segment'), may hold values from -0.0625 to 0.0625
- w_up: bfloat16 [16, 16, 9216], P('segment'), may hold values from -0.375 to 0.375
Outputs:
- grad_down: bfloat16 [16, 9216, 16], P('segment')
- grad_up: bfloat16 [16, 16, 9216], P('segment')
Inputs may be any that keep to these rules, and one draw needn't show every extreme that they name: Each row of sample_ids names every slot 0 to 7 once.
All inputs are finite; a program needn't handle non-finite values.
Results may differ from a plain program's by a relative error of at most 0.04.
Values may be sent and summed in bfloat16 or wider, within the bound.
A program may use at most 128 MiB of HBM per device.

v0:
```python
import jax
import jax.numpy as jnp
from jax import lax
from jax.sharding import PartitionSpec as P


def from_behind(block, axis, distance):
    devices = range(lax.axis_size(axis))
    route = [(i - distance, i) for i in devices if i - distance in devices]
    return lax.ppermute(block, axis, route)


def block_factor(exp_rows):
    magnitude = -exp_rows
    factor = jnp.ones(exp_rows.shape, jnp.float32)
    for bit_pos in range(5):
        factor = jnp.where(
            (magnitude >> bit_pos) % 2 == 1, factor * jnp.float32(0.5 ** (1 << bit_pos)), factor
        )
    return factor


def layer_norm(values, scales):
    center = values - jnp.mean(values, axis=-1, keepdims=True)
    spread = jnp.mean(center * center, axis=-1, keepdims=True)
    return center * lax.rsqrt(spread + 1e-05) * scales


def decode_input(arrived, base_rows, exp_rows):
    row_count = arrived.shape[0]
    blocks = exp_rows.shape[1]
    factor = block_factor(exp_rows)[:, :, None]
    delta_rows = (arrived.astype(jnp.float32) - base_rows.astype(jnp.float32)).reshape(
        row_count, blocks, -1
    )
    scaled = (delta_rows / factor).astype(jnp.bfloat16)
    scaled = lax.optimization_barrier(scaled).astype(jnp.float32)
    clipped = jnp.clip(scaled, -448.0, 448.0)
    return base_rows.astype(jnp.float32) + (clipped * factor).reshape(row_count, -1)


def gelu_tanh(pre_act):
    return jax.nn.gelu(pre_act, approximate=True)


def section_forward(arrived, base_rows, exp_rows, scales, down_proj, up_proj):
    decoded = decode_input(arrived, base_rows, exp_rows)
    normed = layer_norm(decoded, scales).astype(jnp.bfloat16)
    before = jnp.dot(normed, down_proj, preferred_element_type=jnp.float32)
    activated = gelu_tanh(before).astype(jnp.bfloat16)
    output = (decoded + jnp.dot(activated, up_proj, preferred_element_type=jnp.float32)).astype(
        jnp.bfloat16
    )
    return (output, (decoded, normed, before, activated))


def section_backward(grad_out, saved_parts, scales, down_proj, up_proj):
    decoded, normed, before, activated = saved_parts
    grad_upward = jnp.dot(activated.T, grad_out, preferred_element_type=jnp.float32)
    grad_activated = jnp.dot(grad_out, up_proj.T, preferred_element_type=jnp.float32)
    _, gelu_pull = jax.vjp(gelu_tanh, before)
    grad_before = gelu_pull(grad_activated)[0].astype(jnp.bfloat16)
    grad_downward = jnp.dot(normed.T, grad_before, preferred_element_type=jnp.float32)
    grad_normed = jnp.dot(grad_before, down_proj.T, preferred_element_type=jnp.float32)
    _, norm_pull = jax.vjp(lambda inner_rows: layer_norm(inner_rows, scales), decoded)
    grad_decoded = grad_out.astype(jnp.float32) + norm_pull(grad_normed)[0]
    grad_in = grad_decoded.astype(jnp.bfloat16)
    return (grad_in, grad_downward, grad_upward)


def shards(hidden_in, cotangent, stored_bases, sample_ids, block_exps, ln_gains, w_down, w_up):
    section = lax.axis_index("segment")
    sections = lax.axis_size("segment")
    batches = hidden_in.shape[0]
    tok_rows = hidden_in.shape[1]
    features = stored_bases.shape[3]
    low_rank = w_down.shape[2]
    scales = ln_gains[0].astype(jnp.float32)
    down_proj = w_down[0]
    up_proj = w_up[0]
    base_store = stored_bases[0]
    slot_ids = sample_ids[0]
    exps_all = block_exps[0]
    tick_count = batches + sections - 2
    last_section = sections - 1
    zero_rows = jnp.zeros((tok_rows, features), jnp.bfloat16)

    def clamp_batch(batch_raw):
        return jnp.clip(batch_raw, 0, batches - 1)

    def select_batch(batch_pos):
        slot_pos = lax.dynamic_index_in_dim(slot_ids, batch_pos, 0, keepdims=False)
        base_rows = lax.dynamic_index_in_dim(base_store, slot_pos, 0, keepdims=False)
        exp_rows = lax.dynamic_index_in_dim(exps_all, batch_pos, 0, keepdims=False)
        return (base_rows, exp_rows)

    stash_init = (jnp.zeros((batches, tok_rows, features), jnp.bfloat16),)

    def forward_step(tick_pos, arrived_prev, stash_bufs, first_in):
        batch_raw = tick_pos - section
        is_valid = (batch_raw >= 0) & (batch_raw < batches)
        batch_pos = clamp_batch(batch_raw)
        arrived = jnp.where(section == 0, first_in, arrived_prev)
        base_rows, exp_rows = select_batch(batch_pos)
        output, saved_parts = section_forward(
            arrived, base_rows, exp_rows, scales, down_proj, up_proj
        )
        new_items = (arrived,)
        stash_bufs = tuple(
            (
                jnp.where(
                    is_valid,
                    lax.dynamic_update_index_in_dim(buffer, piece_new, batch_pos, 0),
                    buffer,
                )
                for buffer, piece_new in zip(stash_bufs, new_items)
            )
        )
        return (output, stash_bufs)

    def forward_send(tick_pos, loop_state, first_in):
        output, stash_bufs = forward_step(tick_pos, loop_state[0], loop_state[1], first_in)
        return (from_behind(output, "segment", 1), stash_bufs)

    fwd_state = (zero_rows, stash_init)
    full_in, full_cot = (
        lax.all_gather(hidden_in, "segment", axis=2, tiled=True),
        lax.all_gather(cotangent, "segment", axis=2, tiled=True),
    )

    def first_whole(tick_pos):
        return lax.dynamic_index_in_dim(full_in, clamp_batch(tick_pos), 0, keepdims=False)

    fwd_state = lax.fori_loop(
        0,
        tick_count,
        lambda tick_pos, loop_state: forward_send(tick_pos, loop_state, first_whole(tick_pos)),
        fwd_state,
    )
    _, stash_bufs = forward_step(tick_count, fwd_state[0], fwd_state[1], zero_rows)

    def backward_step(tick_pos, grad_prev, acc_down, acc_up, last_cot):
        batch_raw = tick_pos - (last_section - section)
        is_valid = (batch_raw >= 0) & (batch_raw < batches)
        batch_pos = clamp_batch(batch_raw)
        grad_out = jnp.where(section == last_section, last_cot, grad_prev)
        kept_parts = tuple(
            (
                lax.dynamic_index_in_dim(buffer, batch_pos, 0, keepdims=False)
                for buffer in stash_bufs
            )
        )
        base_rows, exp_rows = select_batch(batch_pos)
        _, saved_parts = section_forward(
            kept_parts[0], base_rows, exp_rows, scales, down_proj, up_proj
        )
        grad_in, part_down, part_up = section_backward(
            grad_out, saved_parts, scales, down_proj, up_proj
        )
        weight = is_valid.astype(jnp.float32)
        return (grad_in, acc_down + weight * part_down, acc_up + weight * part_up)

    def backward_send(tick_pos, loop_state, last_cot):
        grad_in, acc_down, acc_up = backward_step(
            tick_pos, loop_state[0], loop_state[1], loop_state[2], last_cot
        )
        return (from_behind(grad_in, "segment", -1), acc_down, acc_up)

    bwd_state = (
        zero_rows,
        jnp.zeros((features, low_rank), jnp.float32),
        jnp.zeros((low_rank, features), jnp.float32),
    )

    def last_whole(tick_pos):
        return lax.dynamic_index_in_dim(full_cot, clamp_batch(tick_pos), 0, keepdims=False)

    bwd_state = lax.fori_loop(
        0,
        tick_count,
        lambda tick_pos, loop_state: backward_send(tick_pos, loop_state, last_whole(tick_pos)),
        bwd_state,
    )
    _, acc_down, acc_up = backward_step(
        tick_count, bwd_state[0], bwd_state[1], bwd_state[2], zero_rows
    )
    total_down, total_up = (
        lax.psum(acc_down.astype(jnp.bfloat16), "dp").astype(jnp.float32),
        lax.psum(acc_up.astype(jnp.bfloat16), "dp").astype(jnp.float32),
    )
    return (total_down.astype(jnp.bfloat16)[None], total_up.astype(jnp.bfloat16)[None])


def solution(mesh):
    return jax.shard_map(
        shards,
        mesh=mesh,
        in_specs=(
            P(None, "dp", "segment"),
            P(None, "dp", "segment"),
            P("segment", None, "dp", None),
            P("dp", None),
            P("segment", None, "dp", None),
            P("segment", None),
            P("segment", None, None),
            P("segment", None, None),
        ),
        out_specs=(P("segment", None, None), P("segment", None, None)),
        check_vma=False,
    )
```

profile of v0, /device:TPU:4, one launch (start us, length us, event | category | flops | bytes accessed | tf_op | source)
XLA Modules:
  0.0 1425.2 jit_solution(3069194866122191592)
XLA Ops:
  7.2 2.8 copy.11
  17.7 129.9 %all-gather.5.cloned.1.call-done = bf16[8,16,9216]{1,0,2:T(8,128)(2,1)} async-done(((bf16[8,16,576]{1,0,2:T(8,128)(2,1)}), bf16[8,16,9216]{1,0,2:T(8,128)(2,1)}) %all-gather.5.cloned.1.call-update) | async-done | bytes 2359312 | tf_op jit(solution)/shard_map/all_gather | solution.py:127
  147.6 17.2 %copy.12 = bf16[8,16,9216]{2,1,0:T(8,128)(2,1)} copy(bf16[8,16,9216]{1,0,2:T(8,128)(2,1)} %all-gather.5.cloned.1.call-done) | data formatting | bytes 4718592 | tf_op jit(solution)/shard_map/while | solution.py:134
  166.5 435.5 %while.37 = (s32[]{:T(128)}, bf16[16,9216]{1,0:T(8,128)(2,1)S(1)}, bf16[8,16,9216]{2,1,0:T(8,128)(2,1)}, s32[]{:T(128)}, s32[8]{0:T(128)}, /*index=5*/bf16[8,16,...) while((s32[]{:T(128)}, bf16[16,9216]{1,0:T(8,128)(2,1)S(1)}, ...), condition=%wide.region_3.4_spmd, body=%wide.region_0.3_spmd.sunk | while | flops 14097053 | bytes 13629206 | solution.py:134
  179.4 7.2 collective-permute-done
  199.3 5.9 collective-permute-done
  218.3 11.8 collective-permute-done
  236.6 2.4 fusion.195
  239.0 3.2 collective-permute-start
  244.2 10.9 collective-permute-done
  261.5 2.4 fusion.195
  263.9 4.1 collective-permute-start
  270.0 4.6 collective-permute-done
  283.4 4.2 collective-permute-start
  289.5 3.7 collective-permute-done
  299.6 2.4 fusion.195
  302.0 5.3 collective-permute-start
  309.3 2.5 collective-permute-done
  320.7 6.2 collective-permute-start
  339.3 7.1 collective-permute-start
  355.4 2.4 fusion.195
  357.9 8.0 collective-permute-start
  376.7 8.7 collective-permute-start
  393.8 2.4 fusion.195
  396.2 8.7 collective-permute-start
  415.7 8.7 collective-permute-start
  435.2 8.7 collective-permute-start
  452.3 2.4 fusion.195
  454.7 8.7 collective-permute-start
  474.3 8.7 collective-permute-start
  493.8 8.7 collective-permute-start
  510.8 2.4 fusion.195
  513.3 8.7 collective-permute-start
  532.8 8.7 collective-permute-start
  549.9 2.4 fusion.195
  552.3 8.7 collective-permute-start
  571.8 8.7 collective-permute-start
  591.3 8.7 collective-permute-start
  608.1 17.2 %copy.13 = bf16[8,16,9216]{2,1,0:T(8,128)(2,1)} copy(bf16[8,16,9216]{1,0,2:T(8,128)(2,1)} %all-gather.3.cloned.1.call-done) | data formatting | bytes 4718592
  626.0 513.2 %while.38 = (s32[]{:T(128)}, bf16[16,9216]{1,0:T(8,128)(2,1)}, f32[9216,16]{0,1:T(8,128)}, f32[16,9216]{1,0:T(8,128)}, pred[]{:T(512)}, /*index=5*/bf16[8,16,921...) while((s32[]{:T(128)}, bf16[16,9216]{1,0:T(8,128)(2,1)}, ...), condition=%wide.region_9.10_spmd.clone, body=%wide.region_4.9_spmd.clone.sunk | while | flops 30912248 | bytes 20785452 | solution.py:178
  643.5 5.2 collective-permute-done.1
  667.6 5.1 collective-permute-done.1
  691.6 4.4 collective-permute-done.1
  714.9 4.4 collective-permute-done.1
  738.2 4.4 collective-permute-done.1
  761.6 4.4 collective-permute-done.1
  784.9 4.4 collective-permute-done.1
  808.2 4.4 collective-permute-done.1
  831.6 4.4 collective-permute-done.1
  854.9 4.4 collective-permute-done.1
  878.2 4.4 collective-permute-done.1
  901.5 4.4 collective-permute-done.1
  924.9 4.4 collective-permute-done.1
  948.2 4.4 collective-permute-done.1
  971.5 4.4 collective-permute-done.1
  994.8 4.4 collective-permute-done.1
  1018.2 4.4 collective-permute-done.1
  1041.5 4.4 collective-permute-done.1
  1064.8 4.4 collective-permute-done.1
  1088.1 4.4 collective-permute-done.1
  1111.5 4.4 collective-permute-done.1
  1134.8 4.4 collective-permute-done.1
  1141.4 2.9 fusion.85
  1144.3 271.0 %all-reduce.3.cloned.1.call-done = (bf16[1,9216,16]{1,2,0:T(8,128)(2,1)}, bf16[1,16,9216]{2,1,0:T(8,128)(2,1)}) async-done(((bf16[1,9216,16]{1,2,0:T(8,128)(2,1)}, bf16[1,16,9216]{2,1,0:T(8,128)(2,1)}), (bf16[1,9216,16]{1,2,0:T(8,128)(2,1)}, bf16[1,16,9216]{2,1,0:T(8,128)(2,1)})) %all-reduce.3.cloned.1.call-update) | async-done | bytes 589840 | tf_op jit(solution)/shard_map/psum | solution.py:188
  (937 shorter events, 571.3 us)
Async XLA Ops:
  7.2 7.4 copy-start.5
  7.2 8.7 copy-start.1
  7.2 140.4 %all-gather.5.cloned.1.call-start = ((), (), s32[]{:S(2)}) async-start(), calls=%async_computation.1 | async-start | bytes 20054016 | tf_op jit(solution)/shard_map/all_gather | solution.py:127
  10.1 598.0 %all-gather.3.cloned.1.call-start = ((), (), s32[]{:S(2)}) async-start(), calls=%async_computation | async-start | bytes 20054016 | tf_op jit(solution)/shard_map/all_gather | solution.py:128
  12.0 1403.3 %all-reduce.3.cloned.1.call-start = ((), (), s32[]{:S(2)}) async-start(), calls=%async_computation.2 | async-start | bytes 1179648 | tf_op jit(solution)/shard_map/psum | solution.py:188
  175.4 11.3 collective-permute-start
  195.5 9.7 collective-permute-start
  214.1 16.0 %collective-permute-start = (bf16[16,9216]{1,0:T(8,128)(2,1)}, bf16[16,9216]{1,0:T(8,128)(2,1)S(1)}, u32[]{:S(2)}, u32[]{:S(2)}) collective-permute-start(bf16[16,9216]{1,0:T(8,128)(2,1)} %fusion.195), channel_id=1, source_target_pairs={{0,32},{32,64},{64,96},{96,128},{128,160},{160,192},{192,224},{224... | collective-permute-start | bytes 884744 | tf_op jit(solution)/shard_map/while/body/eval_jaxpr/ppermute | solution.py:10
  239.0 16.0 %collective-permute-start = (bf16[16,9216]{1,0:T(8,128)(2,1)}, bf16[16,9216]{1,0:T(8,128)(2,1)S(1)}, u32[]{:S(2)}, u32[]{:S(2)}) collective-permute-start(bf16[16,9216]{1,0:T(8,128)(2,1)} %fusion.195), channel_id=1, source_target_pairs={{0,32},{32,64},{64,96},{96,128},{128,160},{160,192},{192,224},{224... | collective-permute-start | bytes 884744 | tf_op jit(solution)/shard_map/while/body/eval_jaxpr/ppermute | solution.py:10
  263.9 10.6 collective-permute-start
  283.4 9.7 collective-permute-start
  302.0 9.7 collective-permute-start
  320.7 9.7 collective-permute-start
  339.3 9.7 collective-permute-start
  357.9 9.9 collective-permute-start
  376.7 10.6 collective-permute-start
  396.2 10.6 collective-permute-start
  415.7 10.6 collective-permute-start
  435.2 10.6 collective-permute-start
  454.7 10.6 collective-permute-start
  474.3 10.6 collective-permute-start
  493.8 10.6 collective-permute-start
  513.3 10.6 collective-permute-start
  532.8 10.6 collective-permute-start
  552.3 10.6 collective-permute-start
  571.8 10.6 collective-permute-start
  591.3 10.6 collective-permute-start
  605.7 19.6 %copy-start.8 = (f32[16]{0:T(128)}, f32[16]{0:T(128)S(1)}, u32[]{:S(2)}) copy-start(f32[16]{0:T(128)S(1)} %broadcast_multiply_fusion.2) | copy-start | bytes 196
  606.1 19.1 %copy-start.9 = (f32[16]{0:T(128)}, f32[16]{0:T(128)S(1)}, u32[]{:S(2)}) copy-start(f32[16]{0:T(128)S(1)} %add_rsqrt_fusion.1) | copy-start | bytes 196
  632.8 4.5 copy-start.7
  638.6 10.1 collective-permute-start.1
  655.5 4.5 copy-start.7
  661.3 11.4 collective-permute-start.1
  679.5 4.5 copy-start.7
  685.2 10.8 collective-permute-start.1
  702.8 4.5 copy-start.7
  708.6 10.8 collective-permute-start.1
  726.1 4.5 copy-start.7
  731.9 10.8 collective-permute-start.1
  749.5 4.5 copy-start.7
  755.2 10.8 collective-permute-start.1
  772.8 4.5 copy-start.7
  778.6 10.8 collective-permute-start.1
  796.1 4.5 copy-start.7
  801.9 10.8 collective-permute-start.1
  819.4 4.5 copy-start.7
  825.2 10.8 collective-permute-start.1
  848.5 10.8 collective-permute-start.1
  871.9 10.8 collective-permute-start.1
  895.2 10.8 collective-permute-start.1
  912.7 4.5 copy-start.7
  918.5 10.8 collective-permute-start.1
  941.8 10.8 collective-permute-start.1
  965.2 10.8 collective-permute-start.1
  988.5 10.8 collective-permute-start.1
  1006.1 4.5 copy-start.7
  1011.8 10.8 collective-permute-start.1
  1029.4 4.5 copy-start.7
  1035.1 10.8 collective-permute-start.1
  1058.5 10.8 collective-permute-start.1
  1081.8 10.8 collective-permute-start.1
  1105.1 10.8 collective-permute-start.1
  1122.7 4.5 copy-start.7
  1128.4 10.8 collective-permute-start.1
  (35 other events, 60.8 us)
Sparse Core Ops, SparseCore 0:
  11.4 136.1 all-gather.4
  150.9 140.3 all-gather.2
  1144.4 270.8 all-reduce.2
where the time goes:
time: 1440 us; the launch traced here: 1430 us
  waiting for transfers between devices  548 us (38%)
  other arithmetic  230 us (16%)
  matrix products  230 us (16%)
  starting transfers between devices  191 us (13%)
  local copies, waits for them, and re-layouts  120 us (8%)
  loops' own time  89.7 us (6%)
  between operations  15.9 us (1%)
    psum x1, waiting for transfers between devices, shards(): lax.psum(acc_down.astype(jnp.bfloat16), 'dp').astype(jnp.float32)  271 us
    ppermute x44, starting transfers between devices, from_behind(): return lax.ppermute(block, axis, route)  191 us
    ppermute x44, waiting for transfers between devices, from_behind(): return lax.ppermute(block, axis, route)  147 us
    all_gather x1, waiting for transfers between devices, shards(): lax.all_gather(hidden_in, 'segment', axis=2, tiled=True)  130 us
    dynamic_slice x45, local copies, waits for them, and re-layouts, select_batch(): slot_pos = lax.dynamic_index_in_dim(slot_ids, batch_pos, 0, keepdims=False)  55.8 us
    dot_general x22, matrix products, section_forward(): jnp.dot(activated, up_proj, preferred_element_type=jnp.float32)  53.5 us
    dot_general x23, matrix products, section_backward(): jnp.dot(normed.T, grad_before, preferred_element_type=jnp.float32)  51.3 us
    dot_general x23, matrix products, section_backward(): jnp.dot(activated.T, grad_out, preferred_element_type=jnp.float32)  49.4 us
  transfers between devices with their start and end apart: 47, of which 33 were waited for; matrix products, arithmetic and copies ran while one was open for 22% of the time, Pallas kernels for 0%

commit v1 on v0

v1 whole, which is shorter than its diff:
```python
import functools

import jax
import jax.numpy as jnp
from jax import lax
from jax.experimental import pallas as pl
from jax.experimental.pallas import tpu as pltpu
from jax.sharding import PartitionSpec as P

MESH = pl.DeviceIdType.MESH
F32 = jnp.float32
BF16 = jnp.bfloat16
NSEC = 16
UNITS = 16
NCH = 8
CH = 1152
WIDTH = NCH * CH
PART = 576
NZ = 16
ROWS = 64
AHEAD = 16
NT = (((1,), (1,)), ((), ()))
TN = (((0,), (0,)), ((), ()))
K_GELU = 0.7978845608028654
C_GELU = 0.044715


def dot(a, b, dims=(((1,), (0,)), ((), ()))):
    return lax.dot_general(a, b, dims, preferred_element_type=F32)


def lanes(shape):
    return lax.broadcasted_iota(jnp.int32, shape, len(shape) - 1)


def gelu(x):
    return 0.5 * x * (1.0 + jnp.tanh(K_GELU * (x + C_GELU * x * x * x)))


def gelu_slope(x):
    th = jnp.tanh(K_GELU * (x + C_GELU * x * x * x))
    return 0.5 * (1.0 + th) + 0.5 * x * (1.0 - th * th) * K_GELU * (1.0 + 3.0 * C_GELU * x * x)


def power_of_two(exps):
    factor = jnp.ones(exps.shape, F32)
    for bit in range(5):
        factor = jnp.where(((-exps) >> bit) & 1 == 1, factor * F32(0.5 ** (1 << bit)), factor)
    return factor


def join_parts(ref):
    first = ref[0].reshape(ROWS, 640).astype(F32)
    second = ref[1].reshape(ROWS, 640).astype(F32)
    lane = lanes((ROWS, 128))
    turned = [pltpu.roll(second[:, 128 * i : 128 * i + 128], 64, 1) for i in range(5)]
    tiles = [first[:, 128 * i : 128 * i + 128] for i in range(4)]
    tiles.append(jnp.where(lane < 64, first[:, 512:640], turned[0]))
    for i in range(4):
        tiles.append(jnp.where(lane < 64, turned[i], turned[i + 1]))
    return jnp.concatenate(tiles, axis=1)


def sections_kernel(
    ids_ref, hid_ref, cot_ref, store_ref, exps_ref, gains_ref, wd_ref, wu_ref,
    parts_ref,
    hid_s, cot_s, fac_s, wts_s, aux_s,
    hid_r, cot_r, fac_r, wts_r, aux_r, base_r,
    spread, wu_all, wuc_all, wdc_all, a_ref, g_ref, d_ref, pay, bpad, bef_all, bef_ref, act_ref,
    mean_ref, rstd_ref, xhat_ref,
    stat_s, stat_r, mix_s, mix_r, cw_s, cw_r, gm_ref, xt_ref, gb_s, gb_r,
    sem_hs, sem_hr, sem_cs, sem_cr, sem_data_s, sem_fac, sem_wts, sem_aux, sem_base,
    sem_st_s, sem_st_r, sem_mx_s, sem_mx_r, sem_cw_s, sem_cw_r, sem_gb_s, sem_gb_r,
):
    me = lax.axis_index("segment")
    dp = lax.axis_index("dp")
    y, xh, core = me // 4, (me // 2) % 2, me % 2
    chunk = 2 * y + core

    def seg_of_chunk(q):
        return 4 * (q // 2) + 2 * xh + q % 2

    barrier = pltpu.get_barrier_semaphore()

    def greet(j, _):
        pl.semaphore_signal(
            barrier, inc=1, device_id=(lax.rem(me + j, NSEC), dp), device_id_type=MESH
        )
        return 0

    lax.fori_loop(1, NSEC, greet, 0)

    hid_s[...] = jnp.zeros(hid_s.shape, BF16)
    cot_s[...] = jnp.zeros(cot_s.shape, BF16)
    fac_s[...] = jnp.zeros(fac_s.shape, BF16)
    for slot in range(8):
        batch = jnp.int32(0)
        for k in range(8):
            batch = jnp.maximum(batch, jnp.where(ids_ref[0, k] == slot, k, 0))
        hid_s[slot, :, 0:PART] = hid_ref[batch]
        cot_s[slot, :, 0:PART] = cot_ref[batch]
        fac_s[slot, :, 0:72] = power_of_two(exps_ref[batch]).astype(BF16)
    lane16 = lanes((UNITS, 128))
    aux = jnp.zeros((UNITS, 128), F32)
    up_total = jnp.zeros((UNITS, 1), F32)
    down_total = jnp.zeros((UNITS, 1), F32)
    for q in range(NCH):
        part = slice(q * CH, (q + 1) * CH)
        scaled = (wd_ref[:, part].astype(F32) * gains_ref[:, part].astype(F32)).astype(BF16)
        wts_s[0:UNITS, part] = scaled
        up = wu_ref[:, part]
        wts_s[UNITS : 2 * UNITS, part] = up
        down_sum = jnp.sum(scaled.astype(F32), axis=1, keepdims=True)
        aux = aux + jnp.where(lane16 == 16 + q, down_sum, 0.0)
        down_total = down_total + down_sum
        up_total = up_total + jnp.sum(up.astype(F32), axis=1, keepdims=True)
    aux = aux + jnp.where(lane16 == 0, down_total * (1.0 / WIDTH), 0.0)
    aux_s[...] = aux + jnp.where(lane16 == 1, up_total * (1.0 / WIDTH), 0.0)

    pl.semaphore_wait(barrier, NSEC - 1)

    def part_copy(x_to, src, dst, send, recv, go):
        target = 4 * y + 2 * x_to + xh
        rows = src.at[4 * x_to : 4 * x_to + 4]

        if go:

            @pl.when(target == me)
            def _():
                pltpu.make_async_copy(rows, dst.at[core], recv.at[core]).start()

        @pl.when(target != me)
        def _():
            copy = pltpu.make_async_remote_copy(
                src_ref=rows, dst_ref=dst.at[core], send_sem=send.at[x_to],
                recv_sem=recv.at[core], device_id=(target, dp), device_id_type=MESH,
            )
            copy.start() if go else copy.wait_send()

    for x_to in range(2):
        part_copy(x_to, hid_s, hid_r, sem_hs, sem_hr, True)

    def data_copies(j):
        target = lax.rem(me + j, NSEC)
        to_chunk = 2 * (target // 4) + target % 2
        slots = pl.ds(4 * ((target // 2) % 2), 4)
        cols = pl.ds(pl.multiple_of(to_chunk * CH, 128), CH)
        pairs = (
            (fac_s.at[slots], fac_r.at[me], sem_fac),
            (aux_s, aux_r.at[me], sem_aux),
            (wts_s.at[:, cols], wts_r.at[me], sem_wts),
            (store_ref.at[slots, :, cols], base_r.at[me], sem_base),
        )
        return [
            pltpu.make_async_remote_copy(
                src_ref=src, dst_ref=dst, send_sem=sem_data_s.at[i, j], recv_sem=sem.at[me],
                device_id=(target, dp), device_id_type=MESH,
            )
            for i, (src, dst, sem) in enumerate(pairs)
        ]

    def send_section():
        slots = pl.ds(4 * xh, 4)
        cols = pl.ds(pl.multiple_of(chunk * CH, 128), CH)
        for src, dst, sem in (
            (fac_s.at[slots], fac_r.at[me], sem_fac),
            (aux_s, aux_r.at[me], sem_aux),
            (wts_s.at[:, cols], wts_r.at[me], sem_wts),
            (store_ref.at[slots, :, cols], base_r.at[me], sem_base),
        ):
            pltpu.make_async_copy(src, dst, sem.at[me]).start()

        def one(j, _):
            for copy in data_copies(j):
                copy.start()
            return 0

        lax.fori_loop(1, NSEC, one, 0)

    @pl.when(me < AHEAD)
    def _():
        send_section()

    for x_to in range(2):
        part_copy(x_to, cot_s, cot_r, sem_cs, sem_cr, True)

    block = lax.broadcasted_iota(jnp.int32, (128, CH), 0)
    feature = lax.broadcasted_iota(jnp.int32, (128, CH), 1)
    spread[...] = jnp.where(block == 9 * chunk + feature // 128, 1.0, 0.0).astype(BF16)
    pay[...] = jnp.zeros(pay.shape, F32)
    bpad[...] = jnp.zeros(bpad.shape, F32)
    bef_all[...] = jnp.zeros(bef_all.shape, F32)
    wuc_all[...] = jnp.zeros(wuc_all.shape, BF16)

    for h in range(2):
        pltpu.make_async_copy(hid_r.at[h], hid_r.at[h], sem_hr.at[h]).wait()
    a_ref[...] = join_parts(hid_r)

    lane = lanes((ROWS, 128))

    def stat_copy(s, j):
        target = seg_of_chunk(lax.rem(chunk + j, NCH))
        return pltpu.make_async_remote_copy(
            src_ref=stat_s.at[s], dst_ref=stat_r.at[s, j - 1], send_sem=sem_st_s.at[s, j - 1],
            recv_sem=sem_st_r.at[s, j - 1], device_id=(target, dp), device_id_type=MESH,
        )

    def mix_copy(s, j):
        to_chunk = lax.rem(chunk + j, NCH)
        return pltpu.make_async_remote_copy(
            src_ref=mix_s.at[s, to_chunk], dst_ref=mix_r.at[s, j - 1],
            send_sem=sem_mx_s.at[s, j - 1], recv_sem=sem_mx_r.at[s, j - 1],
            device_id=(seg_of_chunk(to_chunk), dp), device_id_type=MESH,
        )

    def side_work(s):
        xhat = ((d_ref[...] - mean_ref[s]) * rstd_ref[s]).astype(BF16)
        xhat_ref[s] = xhat
        ups = wuc_all[...]
        rows = dot(xhat, ups, NT)
        gram = dot(wdc_all[s], ups, NT)
        for q in range(NCH):
            mix_s[s, q, 0:8] = rows[8 * q : 8 * q + 8]
            mix_s[s, q, 8:24] = gram
        for j in range(1, NCH):
            mix_copy(s, j).start()
        bpad[:, 0:UNITS] = bef_ref[s]
        bef_all[s // 8] = bef_all[s // 8] + pltpu.roll(bpad[...], 16 * (s % 8), 1)

    def step(s, _):
        @pl.when(me == s + AHEAD)
        def _():
            send_section()

        for ref, sem in ((fac_r, sem_fac), (aux_r, sem_aux), (wts_r, sem_wts), (base_r, sem_base)):
            pltpu.make_async_copy(ref.at[s], ref.at[s], sem.at[s]).wait()
        small = fac_r[s].reshape(ROWS, 128)
        wide = small.astype(F32)
        inverse = jnp.where(wide > 0.0, 1.0 / jnp.where(wide > 0.0, wide, 1.0), 0.0).astype(BF16)
        factor = dot(small, spread[...])
        scale = dot(inverse, spread[...])
        base = base_r[s].reshape(ROWS, CH).astype(F32)
        coded = ((a_ref[...] - base) * scale).astype(BF16).astype(F32)
        decoded = base + jnp.clip(coded, -448.0, 448.0) * factor
        own_mean = jnp.sum(decoded, axis=1, keepdims=True) * (1.0 / CH)
        center = decoded - own_mean
        own_m2 = jnp.sum(center * center, axis=1, keepdims=True)
        pay[:, 0:UNITS] = dot(center.astype(BF16), wts_r[s, 0:UNITS, :], NT)
        row = jnp.where(lane == 16 + chunk, own_mean, pay[...])
        row = jnp.where(lane == 24, own_m2, row)
        packed = row[0:16]
        for g in range(1, 4):
            packed = packed + pltpu.roll(row[16 * g : 16 * g + 16], 32 * g, 1)
        stat_s[s] = packed
        for j in range(1, NCH):
            stat_copy(s, j).start()

        @pl.when(s > 0)
        def _():
            side_work(s - 1)

        d_ref[...] = decoded
        up = wts_r[s, UNITS : 2 * UNITS, :]
        wu_all[pl.ds(pl.multiple_of(s * UNITS, UNITS), UNITS), :] = up
        wuc_all[pl.ds(pl.multiple_of(s * UNITS, UNITS), UNITS), :] = (
            up.astype(F32) - aux_r[s, :, 1:2]
        ).astype(BF16)
        wdc_all[s] = (wts_r[s, 0:UNITS, :].astype(F32) - aux_r[s, :, 0:1]).astype(BF16)

        for j in range(1, NCH):
            stat_copy(s, j).wait_recv()
        total = stat_s[s]
        for j in range(NCH - 1):
            total = total + stat_r[s, j]
        rows = jnp.concatenate(
            [total] + [pltpu.roll(total, 128 - 32 * g, 1) for g in range(1, 4)], axis=0
        )
        is_mean = (lane >= 16) & (lane < 24)
        mean = jnp.sum(jnp.where(is_mean, rows, 0.0), axis=1, keepdims=True) * (1.0 / NCH)
        off = jnp.where(is_mean, rows - mean, 0.0)
        spread_sum = jnp.sum(
            jnp.where(lane == 24, rows, 0.0) + CH * off * off, axis=1, keepdims=True
        )
        rstd = lax.rsqrt(spread_sum * (1.0 / WIDTH) + 1e-05)
        shift = dot(off.astype(BF16), aux_r[s].astype(BF16), NT)
        before = (rows[:, 0:UNITS] + shift) * rstd
        act = gelu(before).astype(BF16)
        a_ref[...] = (decoded + dot(act, up)).astype(BF16).astype(F32)
        bef_ref[s] = before
        act_ref[s] = act
        mean_ref[s] = mean
        rstd_ref[s] = rstd
        return 0

    lax.fori_loop(0, NSEC, step, 0)
    side_work(NSEC - 1)

    for h in range(2):
        pltpu.make_async_copy(cot_r.at[h], cot_r.at[h], sem_cr.at[h]).wait()
    cot = join_parts(cot_r)
    g_ref[...] = cot
    cw_s[...] = dot(cot.astype(BF16), wu_all[...], NT)

    def cw_copy(j):
        to_chunk = lax.rem(chunk + j, NCH)
        return pltpu.make_async_remote_copy(
            src_ref=cw_s.at[pl.ds(pl.multiple_of(8 * to_chunk, 8), 8)], dst_ref=cw_r.at[j - 1],
            send_sem=sem_cw_s.at[j - 1], recv_sem=sem_cw_r.at[j - 1],
            device_id=(seg_of_chunk(to_chunk), dp), device_id_type=MESH,
        )

    for j in range(1, NCH):
        cw_copy(j).start()

    mine = pl.ds(pl.multiple_of(8 * chunk, 8), 8)

    def fold(t, _):
        for j in range(1, NCH):
            mix_copy(t, j).wait_recv()
        both = mix_s[t, chunk]
        for j in range(NCH - 1):
            both = both + mix_r[t, j]
        both = jnp.where(lanes((24, 256)) < UNITS * t, both, 0.0)
        xt_ref[t] = both[0:8]
        gm_ref[pl.ds(pl.multiple_of(t * UNITS, UNITS), UNITS), :] = both[8:24].astype(BF16)
        return 0

    lax.fori_loop(0, NSEC, fold, 0)
    bef8 = jnp.concatenate([bef_all[0, mine, :], bef_all[1, mine, :]], axis=1)
    slope8 = gelu_slope(bef8)
    lane8 = lanes((8, 256))
    for j in range(1, NCH):
        cw_copy(j).wait_recv()
    grad_act = cw_s[mine, :]
    for j in range(NCH - 1):
        grad_act = grad_act + cw_r[j]

    def back(i, carry):
        grad_act, out = carry
        t = NSEC - 1 - i
        here = (lane8 >= UNITS * t) & (lane8 < UNITS * t + UNITS)
        grad_bef = jnp.where(here, grad_act * slope8, 0.0).astype(BF16)
        wide = grad_bef.astype(F32)
        c2 = jnp.sum(wide * bef8, axis=1, keepdims=True) * (1.0 / WIDTH)
        change = dot(grad_bef, gm_ref[...]) - c2 * xt_ref[t]
        return grad_act + rstd_ref[t, mine, :] * change, out + wide

    _, grad_bef = lax.fori_loop(0, NSEC, back, (grad_act, jnp.zeros((8, 256), F32)))
    gb_s[0] = grad_bef[:, 0:128]
    gb_s[1] = grad_bef[:, 128:256]

    def gb_copy(j):
        target = seg_of_chunk(lax.rem(chunk + j, NCH))
        return pltpu.make_async_remote_copy(
            src_ref=gb_s, dst_ref=gb_r.at[:, mine], send_sem=sem_gb_s.at[j - 1],
            recv_sem=sem_gb_r.at[j - 1], device_id=(target, dp), device_id_type=MESH,
        )

    for j in range(1, NCH):
        gb_copy(j).start()
    gb_r[0, mine, :] = grad_bef[:, 0:128]
    gb_r[1, mine, :] = grad_bef[:, 128:256]
    for j in range(1, NCH):
        gb_copy(j).wait_recv()

    def grads(i, _):
        t = NSEC - 1 - i
        turned = pltpu.roll(gb_r[t // 8], lax.rem(128 - 16 * (t % 8), 128), 1)[:, 0:UNITS]
        grad_bef = turned.astype(BF16)
        g = g_ref[...]
        xhat = xhat_ref[t]
        to, at = (t // 2) % 2, 2 * (t // 4) + t % 2
        parts_ref[to, 0, at] = dot(grad_bef, xhat, TN).astype(BF16)
        parts_ref[to, 1, at] = dot(act_ref[t], g.astype(BF16), TN).astype(BF16)
        c2 = jnp.sum(turned * bef_ref[t], axis=1, keepdims=True) * (1.0 / WIDTH)
        g_ref[...] = g + rstd_ref[t] * (dot(grad_bef, wdc_all[t]) - xhat.astype(F32) * c2)
        return 0

    lax.fori_loop(0, NSEC, grads, 0)

    for x_to in range(2):
        part_copy(x_to, hid_s, hid_r, sem_hs, sem_hr, False)
        part_copy(x_to, cot_s, cot_r, sem_cs, sem_cr, False)

    def data_left(j, _):
        for copy in data_copies(j):
            copy.wait_send()
        return 0

    lax.fori_loop(1, NSEC, data_left, 0)

    def group_left(s, _):
        for j in range(1, NCH):
            stat_copy(s, j).wait_send()
            mix_copy(s, j).wait_send()
        return 0

    lax.fori_loop(0, NSEC, group_left, 0)
    for j in range(1, NCH):
        cw_copy(j).wait_send()
        gb_copy(j).wait_send()


def sections_call(ids, hid, cot, store, exps, gains, wd, wu):
    vmem = pl.BlockSpec(memory_space=pltpu.VMEM)
    dma = pltpu.SemaphoreType.DMA
    return pl.pallas_call(
        sections_kernel,
        name="sections",
        out_shape=jax.ShapeDtypeStruct((2, 2, NCH, UNITS, CH), BF16),
        in_specs=[pl.BlockSpec(memory_space=pltpu.SMEM), vmem, vmem,
                  pl.BlockSpec(memory_space=pl.ANY), vmem, vmem, vmem, vmem],
        out_specs=vmem,
        scratch_shapes=[
            pltpu.VMEM((8, 16, 640), BF16), pltpu.VMEM((8, 16, 640), BF16),
            pltpu.VMEM((8, 16, 128), BF16), pltpu.VMEM((2 * UNITS, WIDTH), BF16),
            pltpu.VMEM((UNITS, 128), F32),
            pltpu.VMEM((2, 4, 16, 640), BF16), pltpu.VMEM((2, 4, 16, 640), BF16),
            pltpu.VMEM((NSEC, 4, 16, 128), BF16), pltpu.VMEM((NSEC, 2 * UNITS, CH), BF16),
            pltpu.VMEM((NSEC, UNITS, 128), F32), pltpu.VMEM((NSEC, 4, 16, CH), BF16),
            pltpu.VMEM((128, CH), BF16), pltpu.VMEM((256, CH), BF16), pltpu.VMEM((256, CH), BF16),
            pltpu.VMEM((NSEC, UNITS, CH), BF16), pltpu.VMEM((ROWS, CH), F32),
            pltpu.VMEM((ROWS, CH), F32), pltpu.VMEM((ROWS, CH), F32),
            pltpu.VMEM((ROWS, 128), F32), pltpu.VMEM((ROWS, 128), F32),
            pltpu.VMEM((2, ROWS, 128), F32), pltpu.VMEM((NSEC, ROWS, UNITS), F32),
            pltpu.VMEM((NSEC, ROWS, UNITS), BF16),
            pltpu.VMEM((NSEC, ROWS, 1), F32), pltpu.VMEM((NSEC, ROWS, 1), F32),
            pltpu.VMEM((NSEC, ROWS, CH), BF16),
            pltpu.VMEM((NSEC, 16, 128), F32), pltpu.VMEM((NSEC, NCH - 1, 16, 128), F32),
            pltpu.VMEM((NSEC, NCH, 24, 256), F32), pltpu.VMEM((NSEC, NCH - 1, 24, 256), F32),
            pltpu.VMEM((ROWS, 256), F32), pltpu.VMEM((NCH - 1, 8, 256), F32),
            pltpu.VMEM((256, 256), BF16), pltpu.VMEM((NSEC, 8, 256), F32),
            pltpu.VMEM((2, 8, 128), F32), pltpu.VMEM((2, ROWS, 128), F32),
            dma((2,)), dma((2,)), dma((2,)), dma((2,)), dma((4, NSEC)),
            dma((NSEC,)), dma((NSEC,)), dma((NSEC,)), dma((NSEC,)),
            dma((NSEC, NCH - 1)), dma((NSEC, NCH - 1)), dma((NSEC, NCH - 1)), dma((NSEC, NCH - 1)),
            dma((NCH - 1,)), dma((NCH - 1,)), dma((NCH - 1,)), dma((NCH - 1,)),
        ],
        compiler_params=pltpu.CompilerParams(
            collective_id=1, has_side_effects=True, vmem_limit_bytes=56 * 2**20
        ),
    )(ids, hid, cot, store, exps, gains, wd, wu)


def reduce_kernel(
    parts_ref, gains_ref, down_ref, up_ref,
    x_r, z_s, z_r, f_s, a_r, b_r,
    sem_xs, sem_xr, sem_zs, sem_zr, sem_as, sem_ar, sem_bs, sem_br,
):
    me = lax.axis_index("segment")
    dp = lax.axis_index("dp")
    y, xh, core = me // 4, (me // 2) % 2, me % 2
    z, xl = dp // 2, dp % 2
    chunk = 2 * y + core

    def seg_of(q):
        return 4 * (q // 2) + 2 * xh + q % 2

    goal = seg_of(z // 2)
    near = [(a, b) for a in range(2) for b in range(2) if (a, b) != (0, 0)]

    def x_device(a, b):
        return (4 * y + 2 * lax.rem(xh + a, 2) + core, 2 * z + lax.rem(xl + b, 2))

    barrier = pltpu.get_barrier_semaphore()

    def greet(device):
        pl.semaphore_signal(barrier, inc=1, device_id=device, device_id_type=MESH)

    for a, b in near:
        greet(x_device(a, b))

    def greet_z(j, _):
        greet((me, 2 * lax.rem(z + j, NZ) + xl))
        return 0

    lax.fori_loop(1, NZ, greet_z, 0)

    def greet_goal(j, _):
        @pl.when((goal != me) | (j != z))
        def _():
            greet((goal, 2 * j + xl))

        source, at = seg_of(j // 2), 2 * chunk + j % 2

        @pl.when((source != me) | (at != z))
        def _():
            greet((source, 2 * at + xl))

        return 0

    lax.fori_loop(0, NZ, greet_goal, 0)
    pl.semaphore_wait(
        barrier, len(near) + NZ - 1 + 2 * NZ - 2 * jnp.where(goal == me, 1, 0)
    )

    def x_copy(k, i):
        a, b = near[k]
        to_xh, to_xl = lax.rem(xh + a, 2), lax.rem(xl + b, 2)
        return pltpu.make_async_remote_copy(
            src_ref=parts_ref.at[to_xh, to_xl, i], dst_ref=x_r.at[k, i],
            send_sem=sem_xs.at[k, i], recv_sem=sem_xr.at[k, i],
            device_id=x_device(a, b), device_id_type=MESH,
        )

    def x_send(n, _):
        for k in range(3):
            x_copy(k, NCH - 1 - n).start()
        return 0

    lax.fori_loop(0, NCH, x_send, 0)

    def z_copy(i, h):
        to = 2 * i + h
        step = lax.rem(to - z + NZ, NZ)
        return to, pltpu.make_async_remote_copy(
            src_ref=z_s.at[i, :, 512 * h : 512 * h + 640], dst_ref=z_r.at[step],
            send_sem=sem_zs.at[to], recv_sem=sem_zr.at[step],
            device_id=(me, 2 * to + xl), device_id_type=MESH,
        )

    def z_send(n, _):
        i = NCH - 1 - n
        total = parts_ref[xh, xl, i].astype(F32)
        for k in range(3):
            x_copy(k, i).wait_recv()
            total = total + x_r[k, i].astype(F32)
        z_s[i] = total.astype(BF16)
        for h in range(2):
            to, copy = z_copy(i, h)

            @pl.when(to != z)
            def _():
                copy.start()

        return 0

    lax.fori_loop(0, NCH, z_send, 0)
    f_total = z_s[z // 2, :, pl.ds(pl.multiple_of(512 * (z % 2), 128), 640)].astype(F32)

    def z_recv(step, total):
        pltpu.make_async_copy(z_r.at[step], z_r.at[step], sem_zr.at[step]).wait()
        return total + z_r[step].astype(F32)

    f_s[...] = lax.fori_loop(1, NZ, z_recv, f_total).astype(BF16)

    half = z % 2

    def a_copy(to):
        return pltpu.make_async_remote_copy(
            src_ref=f_s, dst_ref=a_r.at[chunk, half], send_sem=sem_as.at[to],
            recv_sem=sem_ar.at[chunk, half], device_id=(goal, 2 * to + xl), device_id_type=MESH,
        )

    def a_send(j, _):
        to = lax.rem(z + j, NZ)

        @pl.when((goal != me) | (to != z))
        def _():
            a_copy(to).start()

        @pl.when((goal == me) & (to == z))
        def _():
            pltpu.make_async_copy(f_s, a_r.at[chunk, half], sem_ar.at[chunk, half]).start()

        return 0

    lax.fori_loop(0, NZ, a_send, 0)

    def b_copy(q, h):
        return pltpu.make_async_remote_copy(
            src_ref=a_r.at[q, h], dst_ref=b_r.at[q, h], send_sem=sem_bs.at[q, h],
            recv_sem=sem_br.at[q, h], device_id=(me, 2 * z + 1 - xl), device_id_type=MESH,
        )

    for q in range(NCH):
        for h in range(2):
            pltpu.make_async_copy(a_r.at[q, h], a_r.at[q, h], sem_ar.at[q, h]).wait()
            b_copy(q, h).start()

    for q in range(NCH):
        for h in range(2):
            b_copy(q, h).wait_recv()
            low, cols = (0, slice(CH * q, CH * q + 640)) if h == 0 else (
                128, slice(CH * q + 640, CH * q + CH))
            own, other = a_r[q, h][:, low:], b_r[q, h][:, low:]
            down = jnp.where(xl == 0, own, other)
            up_ref[:, cols] = jnp.where(xl == 0, other, own)
            down_ref[:, cols] = (down.astype(F32) * gains_ref[:, cols].astype(F32)).astype(BF16)

    def x_left(i, _):
        for k in range(3):
            x_copy(k, i).wait_send()
        for h in range(2):
            to, copy = z_copy(i, h)

            @pl.when(to != z)
            def _():
                copy.wait_send()

        return 0

    lax.fori_loop(0, NCH, x_left, 0)

    def a_left(to, _):
        @pl.when((goal != me) | (to != z))
        def _():
            a_copy(to).wait_send()

        return 0

    lax.fori_loop(0, NZ, a_left, 0)
    for q in range(NCH):
        for h in range(2):
            b_copy(q, h).wait_send()


def reduce_call(parts, gains):
    vmem = pl.BlockSpec(memory_space=pltpu.VMEM)
    dma = pltpu.SemaphoreType.DMA
    out = jax.ShapeDtypeStruct((UNITS, WIDTH), BF16)
    return pl.pallas_call(
        reduce_kernel,
        name="reduce",
        out_shape=(out, out),
        in_specs=[vmem, vmem],
        out_specs=(vmem, vmem),
        scratch_shapes=[
            pltpu.VMEM((3, NCH, UNITS, CH), BF16), pltpu.VMEM((NCH, UNITS, CH), BF16),
            pltpu.VMEM((NZ, UNITS, 640), BF16), pltpu.VMEM((UNITS, 640), BF16),
            pltpu.VMEM((NCH, 2, UNITS, 640), BF16), pltpu.VMEM((NCH, 2, UNITS, 640), BF16),
            dma((3, NCH)), dma((3, NCH)), dma((NZ,)), dma((NZ,)), dma((NZ,)), dma((NCH, 2)),
            dma((NCH, 2)), dma((NCH, 2)),
        ],
        compiler_params=pltpu.CompilerParams(
            collective_id=2, has_side_effects=True, vmem_limit_bytes=56 * 2**20
        ),
    )(parts, gains)


def shards(hidden_in, cotangent, stored_bases, sample_ids, block_exps, ln_gains, w_down, w_up):
    parts = sections_call(
        sample_ids, hidden_in, cotangent, stored_bases[0], block_exps[0], ln_gains,
        jnp.swapaxes(w_down[0], 0, 1), w_up[0],
    )
    down, up = reduce_call(parts, ln_gains)
    return jnp.swapaxes(down, 0, 1)[None], up[None]


def solution(mesh):
    return jax.shard_map(
        shards,
        mesh=mesh,
        in_specs=(
            P(None, "dp", "segment"),
            P(None, "dp", "segment"),
            P("segment", None, "dp", None),
            P("dp", None),
            P("segment", None, "dp", None),
            P("segment", None),
            P("segment", None, None),
            P("segment", None, None),
        ),
        out_specs=(P("segment", None, None), P("segment", None, None)),
        check_vma=False,
    )
```

time: 1440 us -> 233 us (0.16)
  the two profiles are of different devices: /device:TPU:4 before, /device:TPU:1 now
where the time goes in v1:
time: 233 us; the launch traced here: 232 us
  Pallas kernels  228 us (98%)
  local copies, waits for them, and re-layouts  3.39 us (1%)
    pallas_call x1, Pallas kernels, sections_call(): pl.pallas_call(sections_kernel, name='sections', out_shape=jax.ShapeDtype...  157 us
    pallas_call x1, Pallas kernels, reduce_call(): pl.pallas_call(reduce_kernel, name='reduce', out_shape=(out, out), in_spe...  71.2 us

profile of v1, /device:TPU:1, one launch (start us, length us, event | category | flops | bytes accessed | tf_op | source)
XLA Modules:
  0.0 232.1 jit_solution(11484160449782384247)
XLA Ops:
  0.6 156.9 %sections.1.parts_ref = bf16[2,2,8,16,1152]{4,3,2,1,0:T(8,128)(2,1)} custom-call(s32[1,8]{1,0:T(1,128)} %ids_ref.1, bf16[8,16,576]{2,1,0:T(8,128)(2,1)} %hid_ref.1, bf16[8,16,576]{2,1,0:T(8,128)(2,1)} %cot_ref.1, bf16[8,16,9216]{2,1,0:T(8,128)(2,1)} %bitcast.10, s32[8,16,72]{2,1,0:T(8,128)} %bitcast.15, bf16[1,9216]{1,0:T(2,128)(2,1)} %gains_ref.3, ...), custom_call_target="tpu_custom_call" | custom-call | tf_op jit(solution)/shard_map/sections/pallas_call | solution.py:407
  157.5 71.2 %reduce.1 = (bf16[16,9216]{1,0:T(8,128)(2,1)}, bf16[16,9216]{1,0:T(8,128)(2,1)}) custom-call(bf16[2,2,8,16,1152]{4,3,2,1,0:T(8,128)(2,1)} %sections.1.parts_ref, bf16[1,9216]{1,0:T(2,128)(2,1)} %gains_ref.3), custom_call_target="tpu_custom_call" | custom-call | tf_op jit(solution)/shard_map/reduce/pallas_call | solution.py:622
  228.7 1.7 copy.12
  230.4 1.7 copy.13

commit v2 on v1

v2 whole, which is shorter than its diff:
```python
import functools

import jax
import jax.numpy as jnp
from jax import lax
from jax.experimental import pallas as pl
from jax.experimental.pallas import tpu as pltpu
from jax.sharding import PartitionSpec as P

MESH = pl.DeviceIdType.MESH
F32 = jnp.float32
BF16 = jnp.bfloat16
NSEC = 16
UNITS = 16
NCH = 8
CH = 1152
WIDTH = NCH * CH
PART = 576
NZ = 16
ROWS = 64
HALF = 32
NT = (((1,), (1,)), ((), ()))
TN = (((0,), (0,)), ((), ()))
K_GELU = 0.7978845608028654
C_GELU = 0.044715


def dot(a, b, dims=(((1,), (0,)), ((), ()))):
    return lax.dot_general(a, b, dims, preferred_element_type=F32)


def lanes(shape):
    return lax.broadcasted_iota(jnp.int32, shape, len(shape) - 1)


def gelu(x):
    return 0.5 * x * (1.0 + jnp.tanh(K_GELU * (x + C_GELU * x * x * x)))


def gelu_slope(x):
    th = jnp.tanh(K_GELU * (x + C_GELU * x * x * x))
    return 0.5 * (1.0 + th) + 0.5 * x * (1.0 - th * th) * K_GELU * (1.0 + 3.0 * C_GELU * x * x)


def power_of_two(exps):
    factor = jnp.ones(exps.shape, F32)
    for bit in range(5):
        factor = jnp.where(((-exps) >> bit) & 1 == 1, factor * F32(0.5 ** (1 << bit)), factor)
    return factor


def join_parts(ref):
    first = ref[0].reshape(ROWS, 640).astype(F32)
    second = ref[1].reshape(ROWS, 640).astype(F32)
    lane = lanes((ROWS, 128))
    turned = [pltpu.roll(second[:, 128 * i : 128 * i + 128], 64, 1) for i in range(5)]
    tiles = [first[:, 128 * i : 128 * i + 128] for i in range(4)]
    tiles.append(jnp.where(lane < 64, first[:, 512:640], turned[0]))
    for i in range(4):
        tiles.append(jnp.where(lane < 64, turned[i], turned[i + 1]))
    return jnp.concatenate(tiles, axis=1)


def held(ref, sem):
    pltpu.make_async_copy(ref, ref, sem).wait()


def kernel(
    ids_ref, hid_ref, cot_ref, store_ref, exps_ref, gains_ref, wd_ref, wu_ref,
    down_ref, up_ref,
    hid_s, cot_s, wts_s, fx_s, hid_r, cot_r, wts_r, fx_r, base_r,
    spread, factor_ref, scale_ref, wu_all, wuc_all, wdc_all, a_ref, g_ref, d_ref, cen_ref,
    pay, bpad, bef_all, bef_ref, act_ref, mean_ref, rstd_ref, xhat_ref,
    stat_s, stat_r, mix_s, mix_r, cw_s, cw_r, gm_ref, xt_ref, gb_s, gb_r,
    parts, x_r, z_s, z_r, f_s, a_r, b_r,
    sem_hs, sem_hr, sem_cs, sem_cr, sem_ds, sem_fx, sem_wts, sem_base, sem_fw,
    sem_st_s, sem_st_r, sem_mx_s, sem_mx_r, sem_cw_s, sem_cw_r, sem_gb_s, sem_gb_r,
    sem_xs, sem_xr, sem_zs, sem_zr, sem_as, sem_ar, sem_bs, sem_br,
):
    me = lax.axis_index("segment")
    dp = lax.axis_index("dp")
    y, xh, core = me // 4, (me // 2) % 2, me % 2
    z, xl = dp // 2, dp % 2
    chunk = 2 * y + core

    def seg_of(q):
        return 4 * (q // 2) + 2 * xh + q % 2

    goal = seg_of(z // 2)
    mate = 2 * (z + 1 - 2 * (z % 2)) + xl

    barrier = pltpu.get_barrier_semaphore()

    def greet(device):
        pl.semaphore_signal(barrier, inc=1, device_id=device, device_id_type=MESH)

    def greet_lines(j, _):
        greet((lax.rem(me + j, NSEC), dp))
        greet((me, 2 * lax.rem(z + j, NZ) + xl))
        return 0

    lax.fori_loop(1, NSEC, greet_lines, 0)

    def x_device(a, b):
        return (4 * y + 2 * lax.rem(xh + a, 2) + core, 2 * z + lax.rem(xl + b, 2))

    for a, b in ((0, 1), (1, 0), (1, 1)):
        greet(x_device(a, b))

    def greet_goal(j, _):
        @pl.when((goal != me) | (j != z))
        def _():
            greet((goal, 2 * j + xl))

        source, at = seg_of(j // 2), 2 * chunk + j % 2

        @pl.when((source != me) | (at != z))
        def _():
            greet((source, 2 * at + xl))

        return 0

    lax.fori_loop(0, NZ, greet_goal, 0)

    hid_s[...] = jnp.zeros(hid_s.shape, BF16)
    cot_s[...] = jnp.zeros(cot_s.shape, BF16)
    lane16 = lanes((UNITS, 128))
    batches = []
    for slot in range(8):
        batch = jnp.int32(0)
        for k in range(8):
            batch = jnp.maximum(batch, jnp.where(ids_ref[0, k] == slot, k, 0))
        batches.append(batch)
        hid_s[slot, :, 0:PART] = hid_ref[batch]
        cot_s[slot, :, 0:PART] = cot_ref[batch]
    aux = jnp.zeros((UNITS, 128), F32)
    up_total = jnp.zeros((UNITS, 1), F32)
    down_total = jnp.zeros((UNITS, 1), F32)
    for q in range(NCH):
        part = slice(q * CH, (q + 1) * CH)
        scaled = (wd_ref[:, part].astype(F32) * gains_ref[:, part].astype(F32)).astype(BF16)
        wts_s[0:UNITS, part] = scaled
        up = wu_ref[:, part]
        wts_s[UNITS : 2 * UNITS, part] = up
        down_sum = jnp.sum(scaled.astype(F32), axis=1, keepdims=True)
        aux = aux + jnp.where(lane16 == 16 + q, down_sum, 0.0)
        down_total = down_total + down_sum
        up_total = up_total + jnp.sum(up.astype(F32), axis=1, keepdims=True)
    aux = aux + jnp.where(lane16 == 0, down_total * (1.0 / WIDTH), 0.0)
    aux = (aux + jnp.where(lane16 == 1, up_total * (1.0 / WIDTH), 0.0)).astype(BF16)
    bpad[...] = jnp.zeros(bpad.shape, F32)
    for x_to in range(2):
        picks = []
        for g in range(4):
            bpad[0:16, 0:72] = power_of_two(exps_ref[batches[4 * x_to + g]])
            picks.append(bpad[0:16, :])
        for q in range(NCH):
            packed = jnp.zeros((16, 128), F32)
            for g in range(4):
                turned = pltpu.roll(picks[g], (32 * g - 9 * q) % 128, 1)
                packed = jnp.where((lane16 >= 32 * g) & (lane16 < 32 * g + 9), turned, packed)
            fx_s[x_to, q, 0:16] = packed.astype(BF16)
            fx_s[x_to, q, 16:32] = aux

    pl.semaphore_wait(
        barrier, 2 * (NSEC - 1) + 3 + 2 * NZ - 2 * jnp.where(goal == me, 1, 0)
    )

    def part_copy(x_to, src, dst, send, recv, go):
        target = 4 * y + 2 * x_to + xh
        rows = src.at[4 * x_to : 4 * x_to + 4]

        if go:

            @pl.when(target == me)
            def _():
                pltpu.make_async_copy(rows, dst.at[core], recv.at[core]).start()

        @pl.when(target != me)
        def _():
            copy = pltpu.make_async_remote_copy(
                src_ref=rows, dst_ref=dst.at[core], send_sem=send.at[x_to],
                recv_sem=recv.at[core], device_id=(target, dp), device_id_type=MESH,
            )
            copy.start() if go else copy.wait_send()

    for x_to in range(2):
        part_copy(x_to, hid_s, hid_r, sem_hs, sem_hr, True)

    def place(target):
        to_chunk = 2 * (target // 4) + target % 2
        return (target // 2) % 2, to_chunk, pl.ds(pl.multiple_of(to_chunk * CH, 128), CH)

    def data_send(kind):
        def pair(target):
            x_to, to_chunk, cols = place(target)
            if kind == 0:
                return wts_s.at[:, cols], wts_r.at[me], sem_wts.at[me]
            if kind == 1:
                return fx_s.at[x_to, to_chunk], fx_r.at[me], sem_fx.at[me]
            return store_ref.at[pl.ds(4 * x_to, 4), :, cols], base_r.at[me], sem_base.at[me]

        def one(j, _):
            target = lax.rem(me + j, NSEC)
            src, dst, sem = pair(target)
            pltpu.make_async_remote_copy(
                src_ref=src, dst_ref=dst, send_sem=sem_ds.at[kind], recv_sem=sem,
                device_id=(target, dp), device_id_type=MESH,
            ).start()
            return 0

        src, dst, sem = pair(me)
        pltpu.make_async_copy(src, dst, sem).start()
        lax.fori_loop(1, NSEC, one, 0)

    direct = core == z % 2

    @pl.when(direct)
    def _():
        data_send(0)

    data_send(1)
    data_send(2)
    for x_to in range(2):
        part_copy(x_to, cot_s, cot_r, sem_cs, sem_cr, True)

    block = lax.broadcasted_iota(jnp.int32, (128, CH), 0)
    feature = lax.broadcasted_iota(jnp.int32, (128, CH), 1)
    spread[...] = jnp.where(block % 32 == feature // 128, 1.0, 0.0).astype(BF16)
    pay[...] = jnp.zeros(pay.shape, F32)
    bpad[...] = jnp.zeros(bpad.shape, F32)
    bef_all[...] = jnp.zeros(bef_all.shape, F32)
    wuc_all[...] = jnp.zeros(wuc_all.shape, BF16)

    def wts_on(n):
        s = 2 * n + z % 2
        return s, pltpu.make_async_remote_copy(
            src_ref=wts_r.at[s], dst_ref=wts_r.at[s], send_sem=sem_fw.at[n],
            recv_sem=sem_wts.at[s], device_id=(me, mate), device_id_type=MESH,
        )

    def pass_on(n, _):
        s, copy = wts_on(n)
        held(wts_r.at[s], sem_wts.at[s])
        copy.start()
        return 0

    lax.fori_loop(0, NSEC // 2, pass_on, 0)

    for h in range(2):
        held(hid_r.at[h], sem_hr.at[h])
    first = join_parts(hid_r)
    a_ref[0] = first[0:HALF]
    a_ref[1] = first[HALF:ROWS]

    lane = lanes((HALF, 128))
    lane64 = lanes((16, 128))

    def prefetch(s):
        held(fx_r.at[s], sem_fx.at[s])
        packed = fx_r[s, 0:16].astype(F32)
        small = jnp.concatenate(
            [jnp.where((lane64 >= 32 * g) & (lane64 < 32 * g + 9), packed, 0.0) for g in range(4)],
            axis=0,
        )
        inverse = jnp.where(small > 0.0, 1.0 / jnp.where(small > 0.0, small, 1.0), 0.0)
        factor_ref[...] = dot(small.astype(BF16), spread[...])
        scale_ref[...] = dot(inverse.astype(BF16), spread[...])

    def stat_copy(s, h, j):
        target = seg_of(lax.rem(chunk + j, NCH))
        return pltpu.make_async_remote_copy(
            src_ref=stat_s.at[s, h], dst_ref=stat_r.at[s, h, j - 1], send_sem=sem_st_s.at[s, h],
            recv_sem=sem_st_r.at[s, h], device_id=(target, dp), device_id_type=MESH,
        )

    def start(s, h):
        if h == 0:
            held(base_r.at[s], sem_base.at[s])

            @pl.when(s % 2 != z % 2)
            def _():
                held(wts_r.at[s], sem_wts.at[s])

        rows = slice(HALF * h, HALF * h + HALF)
        total = jnp.zeros((HALF, 128), F32)
        for i in range(CH // 128):
            cols = slice(128 * i, 128 * i + 128)
            base = base_r[s, 2 * h : 2 * h + 2, :, cols].reshape(HALF, 128).astype(F32)
            coded = ((a_ref[h, :, cols] - base) * scale_ref[rows, cols]).astype(BF16)
            decoded = base + jnp.clip(coded.astype(F32), -448.0, 448.0) * factor_ref[rows, cols]
            d_ref[s % 2, h, :, cols] = decoded
            total = total + decoded
        own_mean = jnp.sum(total, axis=1, keepdims=True) * (1.0 / CH)
        squares = jnp.zeros((HALF, 128), F32)
        for i in range(CH // 128):
            cols = slice(128 * i, 128 * i + 128)
            center = d_ref[s % 2, h, :, cols] - own_mean
            squares = squares + center * center
            cen_ref[h, :, cols] = center.astype(BF16)
        own_m2 = jnp.sum(squares, axis=1, keepdims=True)
        pay[h, :, 0:UNITS] = dot(cen_ref[h], wts_r[s, 0:UNITS, :], NT)
        row = jnp.where(lane == 16 + chunk, own_mean, pay[h])
        row = jnp.where(lane == 24, own_m2, row)
        packed = row[0:8]
        for g in range(1, 4):
            packed = packed + pltpu.roll(row[8 * g : 8 * g + 8], 32 * g, 1)
        stat_s[s, h] = packed
        for j in range(1, NCH):
            stat_copy(s, h, j).start()

    def finish(s, h):
        up = wts_r[s, UNITS : 2 * UNITS, :]
        held(stat_r.at[s, h], sem_st_r.at[s, h])
        total = stat_s[s, h]
        for j in range(NCH - 1):
            total = total + stat_r[s, h, j]
        rows = jnp.concatenate(
            [total] + [pltpu.roll(total, 128 - 32 * g, 1) for g in range(1, 4)], axis=0
        )
        is_mean = (lane >= 16) & (lane < 24)
        mean = jnp.sum(jnp.where(is_mean, rows, 0.0), axis=1, keepdims=True) * (1.0 / NCH)
        off = jnp.where(is_mean, rows - mean, 0.0)
        squares = jnp.sum(
            jnp.where(lane == 24, rows, 0.0) + CH * off * off, axis=1, keepdims=True
        )
        rstd = lax.rsqrt(squares * (1.0 / WIDTH) + 1e-05)
        shift = dot(off.astype(BF16), fx_r[s, 16:32], NT)
        before = (rows[:, 0:UNITS] + shift) * rstd
        act = gelu(before).astype(BF16)
        added = dot(act, up)
        a_ref[h] = (d_ref[s % 2, h] + added).astype(BF16).astype(F32)
        here = slice(HALF * h, HALF * h + HALF)
        bef_ref[s, here] = before
        act_ref[s, here] = act
        mean_ref[s, here] = mean
        rstd_ref[s, here] = rstd

    def mix_copy(s, j):
        to_chunk = lax.rem(chunk + j, NCH)
        return pltpu.make_async_remote_copy(
            src_ref=mix_s.at[s, to_chunk], dst_ref=mix_r.at[s, j - 1],
            send_sem=sem_mx_s.at[s], recv_sem=sem_mx_r.at[s],
            device_id=(seg_of(to_chunk), dp), device_id_type=MESH,
        )

    def side_work(s):
        decoded = d_ref[s % 2].reshape(ROWS, CH)
        xhat = ((decoded - mean_ref[s]) * rstd_ref[s]).astype(BF16)
        xhat_ref[s] = xhat
        ups = wuc_all[...]
        rows = dot(xhat, ups, NT)
        downs = (wts_r[s, 0:UNITS, :].astype(F32) - fx_r[s, 16:32, 0:1].astype(F32)).astype(BF16)
        wdc_all[s] = downs
        gram = dot(downs, ups, NT)
        for q in range(NCH):
            mix_s[s, q, 0:8] = rows[8 * q : 8 * q + 8]
            mix_s[s, q, 8:24] = gram
        for j in range(1, NCH):
            mix_copy(s, j).start()
        up = wts_r[s, UNITS : 2 * UNITS, :]
        own = pl.ds(pl.multiple_of(s * UNITS, UNITS), UNITS)
        wu_all[own, :] = up
        wuc_all[own, :] = (up.astype(F32) - fx_r[s, 16:32, 1:2].astype(F32)).astype(BF16)
        bpad[:, 0:UNITS] = bef_ref[s]
        bef_all[s // 8] = bef_all[s // 8] + pltpu.roll(bpad[...], 16 * (s % 8), 1)

    prefetch(0)
    for h in range(2):
        start(0, h)
    prefetch(1)

    def step(s, _):
        for h in range(2):
            finish(s, h)
            start(s + 1, h)
        side_work(s)

        @pl.when(s + 2 < NSEC)
        def _():
            prefetch(s + 2)

        return 0

    lax.fori_loop(0, NSEC - 1, step, 0)

    wu_all[(NSEC - 1) * UNITS : NSEC * UNITS, :] = wts_r[NSEC - 1, UNITS : 2 * UNITS, :]
    for h in range(2):
        held(cot_r.at[h], sem_cr.at[h])
    cot = join_parts(cot_r)
    g_ref[...] = cot
    cw_s[...] = dot(cot.astype(BF16), wu_all[...], NT)

    def cw_copy(j):
        to_chunk = lax.rem(chunk + j, NCH)
        return pltpu.make_async_remote_copy(
            src_ref=cw_s.at[pl.ds(pl.multiple_of(8 * to_chunk, 8), 8)], dst_ref=cw_r.at[j - 1],
            send_sem=sem_cw_s.at[0], recv_sem=sem_cw_r.at[0],
            device_id=(seg_of(to_chunk), dp), device_id_type=MESH,
        )

    for j in range(1, NCH):
        cw_copy(j).start()
    for h in range(2):
        finish(NSEC - 1, h)
    side_work(NSEC - 1)

    mine = pl.ds(pl.multiple_of(8 * chunk, 8), 8)

    def fold(t, _):
        held(mix_r.at[t], sem_mx_r.at[t])
        both = mix_s[t, chunk]
        for j in range(NCH - 1):
            both = both + mix_r[t, j]
        both = jnp.where(lanes((24, 256)) < UNITS * t, both, 0.0)
        xt_ref[t] = both[0:8]
        gm_ref[pl.ds(pl.multiple_of(t * UNITS, UNITS), UNITS), :] = both[8:24].astype(BF16)
        return 0

    held(cw_r, sem_cw_r.at[0])
    grad_act = cw_s[mine, :]
    for j in range(NCH - 1):
        grad_act = grad_act + cw_r[j]
    bef8 = jnp.concatenate([bef_all[0, mine, :], bef_all[1, mine, :]], axis=1)
    slope8 = gelu_slope(bef8)
    lane8 = lanes((8, 256))
    lax.fori_loop(0, NSEC, fold, 0)

    def back(i, carry):
        grad_act, out = carry
        t = NSEC - 1 - i
        here = (lane8 >= UNITS * t) & (lane8 < UNITS * t + UNITS)
        grad_bef = jnp.where(here, grad_act * slope8, 0.0).astype(BF16)
        wide = grad_bef.astype(F32)
        c2 = jnp.sum(wide * bef8, axis=1, keepdims=True) * (1.0 / WIDTH)
        change = dot(grad_bef, gm_ref[...]) - c2 * xt_ref[t]
        return grad_act + rstd_ref[t, mine, :] * change, out + wide

    _, grad_bef = lax.fori_loop(0, NSEC, back, (grad_act, jnp.zeros((8, 256), F32)))
    gb_s[0] = grad_bef[:, 0:128]
    gb_s[1] = grad_bef[:, 128:256]

    def gb_copy(j):
        target = seg_of(lax.rem(chunk + j, NCH))
        return pltpu.make_async_remote_copy(
            src_ref=gb_s, dst_ref=gb_r.at[:, mine], send_sem=sem_gb_s.at[0],
            recv_sem=sem_gb_r.at[0], device_id=(target, dp), device_id_type=MESH,
        )

    for j in range(1, NCH):
        gb_copy(j).start()
    gb_r[0, mine, :] = grad_bef[:, 0:128]
    gb_r[1, mine, :] = grad_bef[:, 128:256]
    held(gb_r.at[:, 0 : ROWS - 8], sem_gb_r.at[0])

    def x_copy(t, kind):
        to, at = (t // 2) % 2, 2 * (t // 4) + t % 2
        a, b = lax.rem(to + xh, 2), lax.rem(kind + xl, 2)
        slot = jnp.maximum(2 * a + b - 1, 0)
        return 2 * a + b, pltpu.make_async_remote_copy(
            src_ref=parts.at[to, kind, at], dst_ref=x_r.at[at, slot], send_sem=sem_xs.at[t, kind],
            recv_sem=sem_xr.at[at], device_id=(4 * y + 2 * to + core, 2 * z + kind),
            device_id_type=MESH,
        )

    def grads(i, _):
        t = NSEC - 1 - i
        to, at = (t // 2) % 2, 2 * (t // 4) + t % 2
        turned = pltpu.roll(gb_r[t // 8], lax.rem(128 - 16 * (t % 8), 128), 1)[:, 0:UNITS]
        grad_bef = turned.astype(BF16)
        g = g_ref[...]
        xhat = xhat_ref[t]
        parts[to, 0, at] = dot(grad_bef, xhat, TN).astype(BF16)
        parts[to, 1, at] = dot(act_ref[t], g.astype(BF16), TN).astype(BF16)
        for kind in range(2):
            away, copy = x_copy(t, kind)

            @pl.when(away > 0)
            def _():
                copy.start()

        c2 = jnp.sum(turned * bef_ref[t], axis=1, keepdims=True) * (1.0 / WIDTH)
        g_ref[...] = g + rstd_ref[t] * (dot(grad_bef, wdc_all[t]) - xhat.astype(F32) * c2)
        return 0

    lax.fori_loop(0, NSEC, grads, 0)

    def z_copy(i, h):
        to = 2 * i + h
        ahead = lax.rem(to - z + NZ, NZ)
        return to, pltpu.make_async_remote_copy(
            src_ref=z_s.at[i, :, 512 * h : 512 * h + 640], dst_ref=z_r.at[ahead],
            send_sem=sem_zs.at[to], recv_sem=sem_zr.at[0],
            device_id=(me, 2 * to + xl), device_id_type=MESH,
        )

    def z_send(n, _):
        i = NCH - 1 - n
        total = parts[xh, xl, i].astype(F32)
        held(x_r.at[i], sem_xr.at[i])
        for k in range(3):
            total = total + x_r[i, k].astype(F32)
        z_s[i] = total.astype(BF16)
        for h in range(2):
            to, copy = z_copy(i, h)

            @pl.when(to != z)
            def _():
                copy.start()

        return 0

    lax.fori_loop(0, NCH, z_send, 0)
    half = z % 2
    f_total = z_s[z // 2, :, pl.ds(pl.multiple_of(512 * half, 128), 640)].astype(F32)
    held(z_r.at[1:NZ], sem_zr.at[0])
    f_s[...] = lax.fori_loop(
        1, NZ, lambda n, total: total + z_r[n].astype(F32), f_total
    ).astype(BF16)

    def a_copy(to):
        return pltpu.make_async_remote_copy(
            src_ref=f_s, dst_ref=a_r.at[chunk, half], send_sem=sem_as.at[to],
            recv_sem=sem_ar.at[chunk, half], device_id=(goal, 2 * to + xl), device_id_type=MESH,
        )

    def a_send(j, _):
        to = lax.rem(z + j, NZ)

        @pl.when((goal != me) | (to != z))
        def _():
            a_copy(to).start()

        @pl.when((goal == me) & (to == z))
        def _():
            pltpu.make_async_copy(f_s, a_r.at[chunk, half], sem_ar.at[chunk, half]).start()

        return 0

    lax.fori_loop(0, NZ, a_send, 0)

    def b_copy(q, h):
        return pltpu.make_async_remote_copy(
            src_ref=a_r.at[q, h], dst_ref=b_r.at[q, h], send_sem=sem_bs.at[q, h],
            recv_sem=sem_br.at[q, h], device_id=(me, 2 * z + 1 - xl), device_id_type=MESH,
        )

    for q in range(NCH):
        for h in range(2):
            held(a_r.at[q, h], sem_ar.at[q, h])
            b_copy(q, h).start()

    for x_to in range(2):
        part_copy(x_to, hid_s, hid_r, sem_hs, sem_hr, False)
        part_copy(x_to, cot_s, cot_r, sem_cs, sem_cr, False)

    @pl.when(direct)
    def _():
        held(wts_r.at[0 : NSEC - 1], sem_ds.at[0])

    held(fx_r.at[0 : NSEC - 1], sem_ds.at[1])
    held(base_r.at[0 : NSEC - 1], sem_ds.at[2])

    def forwarded(n, _):
        wts_on(n)[1].wait_send()
        return 0

    lax.fori_loop(0, NSEC // 2, forwarded, 0)

    def left(s, _):
        for h in range(2):
            held(stat_r.at[s, h], sem_st_s.at[s, h])
        held(mix_r.at[s], sem_mx_s.at[s])
        for kind in range(2):
            away, copy = x_copy(s, kind)

            @pl.when(away > 0)
            def _():
                copy.wait_send()

        return 0

    lax.fori_loop(0, NSEC, left, 0)
    held(cw_r, sem_cw_s.at[0])
    held(gb_r.at[:, 0 : ROWS - 8], sem_gb_s.at[0])

    def z_left(i, _):
        for h in range(2):
            to, copy = z_copy(i, h)

            @pl.when(to != z)
            def _():
                copy.wait_send()

        return 0

    lax.fori_loop(0, NCH, z_left, 0)

    def a_left(to, _):
        @pl.when((goal != me) | (to != z))
        def _():
            a_copy(to).wait_send()

        return 0

    lax.fori_loop(0, NZ, a_left, 0)

    for q in range(NCH):
        for h in range(2):
            b_copy(q, h).wait_recv()
            low, cols = (0, slice(CH * q, CH * q + 640)) if h == 0 else (
                128, slice(CH * q + 640, CH * q + CH))
            own, other = a_r[q, h][:, low:], b_r[q, h][:, low:]
            down = jnp.where(xl == 0, own, other)
            up_ref[:, cols] = jnp.where(xl == 0, other, own)
            down_ref[:, cols] = (down.astype(F32) * gains_ref[:, cols].astype(F32)).astype(BF16)
    for q in range(NCH):
        for h in range(2):
            b_copy(q, h).wait_send()


def whole_call(ids, hid, cot, store, exps, gains, wd, wu):
    vmem = pl.BlockSpec(memory_space=pltpu.VMEM)
    dma = pltpu.SemaphoreType.DMA

    def bf(*shape):
        return pltpu.VMEM(shape, BF16)

    def f32(*shape):
        return pltpu.VMEM(shape, F32)

    out = jax.ShapeDtypeStruct((UNITS, WIDTH), BF16)
    peers = NCH - 1
    return pl.pallas_call(
        kernel,
        name="sections",
        out_shape=(out, out),
        in_specs=[pl.BlockSpec(memory_space=pltpu.SMEM), vmem, vmem,
                  pl.BlockSpec(memory_space=pl.ANY), vmem, vmem, vmem, vmem],
        out_specs=(vmem, vmem),
        scratch_shapes=[
            bf(8, 16, 640), bf(8, 16, 640), bf(2 * UNITS, WIDTH), bf(2, NCH, 32, 128),
            bf(2, 4, 16, 640), bf(2, 4, 16, 640), bf(NSEC, 2 * UNITS, CH), bf(NSEC, 32, 128),
            bf(NSEC, 4, 16, CH),
            bf(128, CH), f32(ROWS, CH), f32(ROWS, CH), bf(256, CH), bf(256, CH),
            bf(NSEC, UNITS, CH), f32(2, HALF, CH), f32(ROWS, CH), f32(2, 2, HALF, CH),
            bf(2, HALF, CH),
            f32(2, HALF, 128), f32(ROWS, 128), f32(2, ROWS, 128), f32(NSEC, ROWS, UNITS),
            bf(NSEC, ROWS, UNITS), f32(NSEC, ROWS, 1), f32(NSEC, ROWS, 1), bf(NSEC, ROWS, CH),
            f32(NSEC, 2, 8, 128), f32(NSEC, 2, peers, 8, 128),
            f32(NSEC, NCH, 24, 256), f32(NSEC, peers, 24, 256),
            f32(ROWS, 256), f32(peers, 8, 256), bf(256, 256), f32(NSEC, 8, 256),
            f32(2, 8, 128), f32(2, ROWS, 128),
            bf(2, 2, NCH, UNITS, CH), bf(NCH, 3, UNITS, CH), bf(NCH, UNITS, CH),
            bf(NZ, UNITS, 640), bf(UNITS, 640), bf(NCH, 2, UNITS, 640), bf(NCH, 2, UNITS, 640),
            dma((2,)), dma((2,)), dma((2,)), dma((2,)), dma((3,)), dma((NSEC,)), dma((NSEC,)),
            dma((NSEC,)), dma((NSEC // 2,)),
            dma((NSEC, 2)), dma((NSEC, 2)), dma((NSEC,)), dma((NSEC,)), dma((1,)), dma((1,)),
            dma((1,)), dma((1,)),
            dma((NSEC, 2)), dma((NCH,)), dma((NZ,)), dma((1,)), dma((NZ,)), dma((NCH, 2)),
            dma((NCH, 2)), dma((NCH, 2)),
        ],
        compiler_params=pltpu.CompilerParams(
            collective_id=1, has_side_effects=True, vmem_limit_bytes=56 * 2**20
        ),
    )(ids, hid, cot, store, exps, gains, wd, wu)


def shards(hidden_in, cotangent, stored_bases, sample_ids, block_exps, ln_gains, w_down, w_up):
    down, up = whole_call(
        sample_ids, hidden_in, cotangent, stored_bases[0], block_exps[0], ln_gains,
        jnp.swapaxes(w_down[0], 0, 1), w_up[0],
    )
    return jnp.swapaxes(down, 0, 1)[None], up[None]


def solution(mesh):
    return jax.shard_map(
        shards,
        mesh=mesh,
        in_specs=(
            P(None, "dp", "segment"),
            P(None, "dp", "segment"),
            P("segment", None, "dp", None),
            P("dp", None),
            P("segment", None, "dp", None),
            P("segment", None),
            P("segment", None, None),
            P("segment", None, None),
        ),
        out_specs=(P("segment", None, None), P("segment", None, None)),
        check_vma=False,
    )
```

time: 233 us -> 197 us (0.85)
  Pallas kernels: 228 us -> 192 us
    pallas_call x2 -> x1, Pallas kernels: 228 us -> 192 us  [whole_call(): pl.pallas_call(kernel, name='sections', out_shape=(out, out), in_specs=[p...]
where the time goes in v2:
time: 197 us; the launch traced here: 196 us
  Pallas kernels  192 us (97%)
  local copies, waits for them, and re-layouts  3.39 us (2%)
    pallas_call x1, Pallas kernels, whole_call(): pl.pallas_call(kernel, name='sections', out_shape=(out, out), in_specs=[p...  192 us

profile of v2, /device:TPU:1, one launch (start us, length us, event | category | flops | bytes accessed | tf_op | source)
XLA Modules:
  0.0 195.8 jit_solution(12058018776836381866)
XLA Ops:
  0.6 191.8 %sections.1 = (bf16[16,9216]{1,0:T(8,128)(2,1)}, bf16[16,9216]{1,0:T(8,128)(2,1)}) custom-call(s32[1,8]{1,0:T(1,128)} %ids_ref.1, bf16[8,16,576]{2,1,0:T(8,128)(2,1)} %hid_ref.1, bf16[8,16,576]{2,1,0:T(8,128)(2,1)} %cot_ref.1, bf16[8,16,9216]{2,1,0:T(8,128)(2,1)} %bitcast.10, s32[8,16,72]{2,1,0:T(8,128)} %bitcast.15, bf16[1,9216]{1,0:T(2,128)(2,1)} %gains_ref.1, ...), custom_call_target="tpu_custom_call" | custom-call | tf_op jit(solution)/shard_map/sections/pallas_call | solution.py:634
  192.4 1.7 copy.12
  194.1 1.7 copy.13

commit v3 on v2

--- a/solution.py
+++ b/solution.py
@@ -71,10 +71,11 @@
     hid_s, cot_s, wts_s, fx_s, hid_r, cot_r, wts_r, fx_r, base_r,
     spread, factor_ref, scale_ref, wu_all, wuc_all, wdc_all, a_ref, g_ref, d_ref, cen_ref,
     pay, bpad, bef_all, bef_ref, act_ref, mean_ref, rstd_ref, xhat_ref,
-    stat_s, stat_r, mix_s, mix_r, cw_s, cw_r, gm_ref, xt_ref, gb_s, gb_r,
+    stat_s, stat_r, mix_s, mix_r, cw_s, cw_r, gram_s, gram_r, gm_ref, xt_ref, gb_s, gb_r,
     parts, x_r, z_s, z_r, f_s, a_r, b_r,
     sem_hs, sem_hr, sem_cs, sem_cr, sem_ds, sem_fx, sem_wts, sem_base, sem_fw,
-    sem_st_s, sem_st_r, sem_mx_s, sem_mx_r, sem_cw_s, sem_cw_r, sem_gb_s, sem_gb_r,
+    sem_st_s, sem_st_r, sem_mx_s, sem_mx_r, sem_cw_s, sem_cw_r, sem_gr_s, sem_gr_r,
+    sem_gm_s, sem_gm_r, sem_gb_s, sem_gb_r,
     sem_xs, sem_xr, sem_zs, sem_zr, sem_as, sem_ar, sem_bs, sem_br,
 ):
     me = lax.axis_index("segment")
@@ -86,6 +87,8 @@
     def seg_of(q):
         return 4 * (q // 2) + 2 * xh + q % 2
 
+    peer_chunks = [lax.rem(chunk + j, NCH) for j in range(NCH)]
+    peer_segs = [seg_of(q) for q in peer_chunks]
     goal = seg_of(z // 2)
     mate = 2 * (z + 1 - 2 * (z % 2)) + xl
 
@@ -230,7 +233,6 @@
     pay[...] = jnp.zeros(pay.shape, F32)
     bpad[...] = jnp.zeros(bpad.shape, F32)
     bef_all[...] = jnp.zeros(bef_all.shape, F32)
-    wuc_all[...] = jnp.zeros(wuc_all.shape, BF16)
 
     def wts_on(n):
         s = 2 * n + z % 2
@@ -257,7 +259,6 @@
     lane64 = lanes((16, 128))
 
     def prefetch(s):
-        held(fx_r.at[s], sem_fx.at[s])
         packed = fx_r[s, 0:16].astype(F32)
         small = jnp.concatenate(
             [jnp.where((lane64 >= 32 * g) & (lane64 < 32 * g + 9), packed, 0.0) for g in range(4)],
@@ -268,7 +269,7 @@
         scale_ref[...] = dot(inverse.astype(BF16), spread[...])
 
     def stat_copy(s, h, j):
-        target = seg_of(lax.rem(chunk + j, NCH))
+        target = peer_segs[j]
         return pltpu.make_async_remote_copy(
             src_ref=stat_s.at[s, h], dst_ref=stat_r.at[s, h, j - 1], send_sem=sem_st_s.at[s, h],
             recv_sem=sem_st_r.at[s, h], device_id=(target, dp), device_id_type=MESH,
@@ -277,10 +278,6 @@
     def start(s, h):
         if h == 0:
             held(base_r.at[s], sem_base.at[s])
-
-            @pl.when(s % 2 != z % 2)
-            def _():
-                held(wts_r.at[s], sem_wts.at[s])
 
         rows = slice(HALF * h, HALF * h + HALF)
         total = jnp.zeros((HALF, 128), F32)
@@ -337,33 +334,80 @@
         rstd_ref[s, here] = rstd
 
     def mix_copy(s, j):
-        to_chunk = lax.rem(chunk + j, NCH)
         return pltpu.make_async_remote_copy(
-            src_ref=mix_s.at[s, to_chunk], dst_ref=mix_r.at[s, j - 1],
-            send_sem=sem_mx_s.at[s], recv_sem=sem_mx_r.at[s],
-            device_id=(seg_of(to_chunk), dp), device_id_type=MESH,
+            src_ref=mix_s.at[s, pl.ds(pl.multiple_of(8 * peer_chunks[j], 8), 8)],
+            dst_ref=mix_r.at[s, j - 1], send_sem=sem_mx_s.at[s], recv_sem=sem_mx_r.at[s],
+            device_id=(peer_segs[j], dp), device_id_type=MESH,
         )
 
     def side_work(s):
         decoded = d_ref[s % 2].reshape(ROWS, CH)
         xhat = ((decoded - mean_ref[s]) * rstd_ref[s]).astype(BF16)
         xhat_ref[s] = xhat
-        ups = wuc_all[...]
-        rows = dot(xhat, ups, NT)
-        downs = (wts_r[s, 0:UNITS, :].astype(F32) - fx_r[s, 16:32, 0:1].astype(F32)).astype(BF16)
-        wdc_all[s] = downs
-        gram = dot(downs, ups, NT)
-        for q in range(NCH):
-            mix_s[s, q, 0:8] = rows[8 * q : 8 * q + 8]
-            mix_s[s, q, 8:24] = gram
+        mix_s[s] = dot(xhat, wuc_all[...], NT)
         for j in range(1, NCH):
             mix_copy(s, j).start()
+        bpad[:, 0:UNITS] = bef_ref[s]
+        bef_all[s // 8] = bef_all[s // 8] + pltpu.roll(bpad[...], 16 * (s % 8), 1)
+
+    def weights(s, _):
+        held(fx_r.at[s], sem_fx.at[s])
+
+        @pl.when(s % 2 != z % 2)
+        def _():
+            held(wts_r.at[s], sem_wts.at[s])
+
         up = wts_r[s, UNITS : 2 * UNITS, :]
         own = pl.ds(pl.multiple_of(s * UNITS, UNITS), UNITS)
         wu_all[own, :] = up
         wuc_all[own, :] = (up.astype(F32) - fx_r[s, 16:32, 1:2].astype(F32)).astype(BF16)
-        bpad[:, 0:UNITS] = bef_ref[s]
-        bef_all[s // 8] = bef_all[s // 8] + pltpu.roll(bpad[...], 16 * (s % 8), 1)
+        wdc_all[s] = (
+            wts_r[s, 0:UNITS, :].astype(F32) - fx_r[s, 16:32, 0:1].astype(F32)
+        ).astype(BF16)
+        return 0
+
+    lax.fori_loop(0, NSEC, weights, 0)
+
+    for h in range(2):
+        held(cot_r.at[h], sem_cr.at[h])
+    cot = join_parts(cot_r)
+    g_ref[...] = cot
+    cw_s[...] = dot(cot.astype(BF16), wu_all[...], NT)
+
+    def cw_copy(j):
+        return pltpu.make_async_remote_copy(
+            src_ref=cw_s.at[pl.ds(pl.multiple_of(8 * peer_chunks[j], 8), 8)],
+            dst_ref=cw_r.at[j - 1],
+            send_sem=sem_cw_s.at[0], recv_sem=sem_cw_r.at[0],
+            device_id=(peer_segs[j], dp), device_id_type=MESH,
+        )
+
+    for j in range(1, NCH):
+        cw_copy(j).start()
+
+    products = dot(wdc_all[...].reshape(256, CH), wuc_all[...], NT)
+    row_sec = lax.broadcasted_iota(jnp.int32, (256, 256), 0) // UNITS
+    col_sec = lanes((256, 256)) // UNITS
+    gram_s[...] = jnp.where(col_sec < row_sec, products, 0.0)
+    own_gram = pl.ds(pl.multiple_of(32 * chunk, 32), 32)
+
+    def gram_copy(j):
+        return pltpu.make_async_remote_copy(
+            src_ref=gram_s.at[pl.ds(pl.multiple_of(32 * peer_chunks[j], 32), 32)],
+            dst_ref=gram_r.at[j - 1],
+            send_sem=sem_gr_s.at[0], recv_sem=sem_gr_r.at[0],
+            device_id=(peer_segs[j], dp), device_id_type=MESH,
+        )
+
+    def gm_copy(j):
+        return pltpu.make_async_remote_copy(
+            src_ref=gm_ref.at[own_gram], dst_ref=gm_ref.at[own_gram],
+            send_sem=sem_gm_s.at[0], recv_sem=sem_gm_r.at[0],
+            device_id=(peer_segs[j], dp), device_id_type=MESH,
+        )
+
+    for j in range(1, NCH):
+        gram_copy(j).start()
 
     prefetch(0)
     for h in range(2):
@@ -380,27 +424,20 @@
         def _():
             prefetch(s + 2)
 
+        @pl.when(s == 3)
+        def _():
+            held(gram_r, sem_gr_r.at[0])
+            total = gram_s[own_gram, :]
+            for j in range(NCH - 1):
+                total = total + gram_r[j]
+            gm_ref[own_gram, :] = total.astype(BF16)
+            for j in range(1, NCH):
+                gm_copy(j).start()
+
         return 0
 
     lax.fori_loop(0, NSEC - 1, step, 0)
 
-    wu_all[(NSEC - 1) * UNITS : NSEC * UNITS, :] = wts_r[NSEC - 1, UNITS : 2 * UNITS, :]
-    for h in range(2):
-        held(cot_r.at[h], sem_cr.at[h])
-    cot = join_parts(cot_r)
-    g_ref[...] = cot
-    cw_s[...] = dot(cot.astype(BF16), wu_all[...], NT)
-
-    def cw_copy(j):
-        to_chunk = lax.rem(chunk + j, NCH)
-        return pltpu.make_async_remote_copy(
-            src_ref=cw_s.at[pl.ds(pl.multiple_of(8 * to_chunk, 8), 8)], dst_ref=cw_r.at[j - 1],
-            send_sem=sem_cw_s.at[0], recv_sem=sem_cw_r.at[0],
-            device_id=(seg_of(to_chunk), dp), device_id_type=MESH,
-        )
-
-    for j in range(1, NCH):
-        cw_copy(j).start()
     for h in range(2):
         finish(NSEC - 1, h)
     side_work(NSEC - 1)
@@ -409,14 +446,13 @@
 
     def fold(t, _):
         held(mix_r.at[t], sem_mx_r.at[t])
-        both = mix_s[t, chunk]
+        both = mix_s[t, mine, :]
         for j in range(NCH - 1):
             both = both + mix_r[t, j]
-        both = jnp.where(lanes((24, 256)) < UNITS * t, both, 0.0)
-        xt_ref[t] = both[0:8]
-        gm_ref[pl.ds(pl.multiple_of(t * UNITS, UNITS), UNITS), :] = both[8:24].astype(BF16)
-        return 0
-
+        xt_ref[t] = jnp.where(lanes((8, 256)) < UNITS * t, both, 0.0)
+        return 0
+
+    held(gm_ref.at[0 : 256 - 32], sem_gm_r.at[0])
     held(cw_r, sem_cw_r.at[0])
     grad_act = cw_s[mine, :]
     for j in range(NCH - 1):
@@ -441,7 +477,7 @@
     gb_s[1] = grad_bef[:, 128:256]
 
     def gb_copy(j):
-        target = seg_of(lax.rem(chunk + j, NCH))
+        target = peer_segs[j]
         return pltpu.make_async_remote_copy(
             src_ref=gb_s, dst_ref=gb_r.at[:, mine], send_sem=sem_gb_s.at[0],
             recv_sem=sem_gb_r.at[0], device_id=(target, dp), device_id_type=MESH,
@@ -582,6 +618,8 @@
 
     lax.fori_loop(0, NSEC, left, 0)
     held(cw_r, sem_cw_s.at[0])
+    held(gram_r, sem_gr_s.at[0])
+    held(gm_ref.at[0 : 256 - 32], sem_gm_s.at[0])
     held(gb_r.at[:, 0 : ROWS - 8], sem_gb_s.at[0])
 
     def z_left(i, _):
@@ -648,15 +686,15 @@
             f32(2, HALF, 128), f32(ROWS, 128), f32(2, ROWS, 128), f32(NSEC, ROWS, UNITS),
             bf(NSEC, ROWS, UNITS), f32(NSEC, ROWS, 1), f32(NSEC, ROWS, 1), bf(NSEC, ROWS, CH),
             f32(NSEC, 2, 8, 128), f32(NSEC, 2, peers, 8, 128),
-            f32(NSEC, NCH, 24, 256), f32(NSEC, peers, 24, 256),
-            f32(ROWS, 256), f32(peers, 8, 256), bf(256, 256), f32(NSEC, 8, 256),
+            f32(NSEC, ROWS, 256), f32(NSEC, peers, 8, 256),
+            f32(ROWS, 256), f32(peers, 8, 256), f32(256, 256), f32(peers, 32, 256), bf(256, 256), f32(NSEC, 8, 256),
             f32(2, 8, 128), f32(2, ROWS, 128),
             bf(2, 2, NCH, UNITS, CH), bf(NCH, 3, UNITS, CH), bf(NCH, UNITS, CH),
             bf(NZ, UNITS, 640), bf(UNITS, 640), bf(NCH, 2, UNITS, 640), bf(NCH, 2, UNITS, 640),
             dma((2,)), dma((2,)), dma((2,)), dma((2,)), dma((3,)), dma((NSEC,)), dma((NSEC,)),
             dma((NSEC,)), dma((NSEC // 2,)),
             dma((NSEC, 2)), dma((NSEC, 2)), dma((NSEC,)), dma((NSEC,)), dma((1,)), dma((1,)),
-            dma((1,)), dma((1,)),
+            dma((1,)), dma((1,)), dma((1,)), dma((1,)), dma((1,)), dma((1,)),
             dma((NSEC, 2)), dma((NCH,)), dma((NZ,)), dma((1,)), dma((NZ,)), dma((NCH, 2)),
             dma((NCH, 2)), dma((NCH, 2)),
         ],

time: 197 us -> 200 us (1.015)
  Pallas kernels: 192 us -> 195 us
    pallas_call x1, Pallas kernels: 192 us -> 195 us  [whole_call(): pl.pallas_call(kernel, name='sections', out_shape=(out, out), in_specs=[p...]
where the time goes in v3:
time: 200 us; the launch traced here: 199 us
  Pallas kernels  195 us (98%)
  local copies, waits for them, and re-layouts  3.39 us (2%)
    pallas_call x1, Pallas kernels, whole_call(): pl.pallas_call(kernel, name='sections', out_shape=(out, out), in_specs=[p...  195 us

profile of v3, /device:TPU:1, one launch (start us, length us, event | category | flops | bytes accessed | tf_op | source)
XLA Modules:
  0.0 198.9 jit_solution(14595246927660841159)
XLA Ops:
  0.6 194.8 %sections.1 = (bf16[16,9216]{1,0:T(8,128)(2,1)}, bf16[16,9216]{1,0:T(8,128)(2,1)}) custom-call(s32[1,8]{1,0:T(1,128)} %ids_ref.1, bf16[8,16,576]{2,1,0:T(8,128)(2,1)} %hid_ref.1, bf16[8,16,576]{2,1,0:T(8,128)(2,1)} %cot_ref.1, bf16[8,16,9216]{2,1,0:T(8,128)(2,1)} %bitcast.10, s32[8,16,72]{2,1,0:T(8,128)} %bitcast.15, bf16[1,9216]{1,0:T(2,128)(2,1)} %gains_ref.1, ...), custom_call_target="tpu_custom_call" | custom-call | tf_op jit(solution)/shard_map/sections/pallas_call | solution.py:672
  195.5 1.7 copy.12
  197.2 1.7 copy.13

commit v4 on v3

--- a/solution.py
+++ b/solution.py
@@ -15,6 +15,10 @@
 NCH = 8
 CH = 1152
 WIDTH = NCH * CH
+SPLIT = (slice(0, 640), slice(640, 1152))
+SIZES = (640, 512)
+PEERS = ((0, 0), (2, 0), (2, 1), (1, 0), (3, 0), (1, 1), (3, 1), (0, 1))
+PARTNERS = (2, 4, 12, 10, 6, 14, 8, 3, 5, 13, 11, 7, 15, 9, 1)
 PART = 576
 NZ = 16
 ROWS = 64
@@ -87,10 +91,10 @@
     def seg_of(q):
         return 4 * (q // 2) + 2 * xh + q % 2
 
-    peer_chunks = [lax.rem(chunk + j, NCH) for j in range(NCH)]
+    peer_chunks = [2 * lax.rem(y + dy, 4) + lax.rem(core + dc, 2) for dy, dc in PEERS]
     peer_segs = [seg_of(q) for q in peer_chunks]
     goal = seg_of(z // 2)
-    mate = 2 * (z + 1 - 2 * (z % 2)) + xl
+    mates = [2 * lax.rem(z + step, NZ) + xl for step in (NZ - 1, 1)]
 
     barrier = pltpu.get_barrier_semaphore()
 
@@ -203,18 +207,30 @@
                 return fx_s.at[x_to, to_chunk], fx_r.at[me], sem_fx.at[me]
             return store_ref.at[pl.ds(4 * x_to, 4), :, cols], base_r.at[me], sem_base.at[me]
 
-        def one(j, _):
-            target = lax.rem(me + j, NSEC)
+        src, dst, sem = pair(me)
+        pltpu.make_async_copy(src, dst, sem).start()
+        for bits in PARTNERS:
+            target = me ^ bits
             src, dst, sem = pair(target)
             pltpu.make_async_remote_copy(
                 src_ref=src, dst_ref=dst, send_sem=sem_ds.at[kind], recv_sem=sem,
                 device_id=(target, dp), device_id_type=MESH,
             ).start()
-            return 0
-
-        src, dst, sem = pair(me)
-        pltpu.make_async_copy(src, dst, sem).start()
-        lax.fori_loop(1, NSEC, one, 0)
+
+    def wts_on(n, k):
+        s = 2 * n + z % 2
+        part = pl.ds(k * UNITS, UNITS)
+        return pltpu.make_async_remote_copy(
+            src_ref=wts_r.at[s, part], dst_ref=wts_r.at[s, part], send_sem=sem_fw.at[n],
+            recv_sem=sem_wts.at[s], device_id=(me, mates[k]), device_id_type=MESH,
+        )
+
+    def pass_on(n, _):
+        s = 2 * n + z % 2
+        held(wts_r.at[s], sem_wts.at[s])
+        for k in range(2):
+            wts_on(n, k).start()
+        return 0
 
     direct = core == z % 2
 
@@ -224,30 +240,16 @@
 
     data_send(1)
     data_send(2)
+    lax.fori_loop(0, NSEC // 2, pass_on, 0)
     for x_to in range(2):
         part_copy(x_to, cot_s, cot_r, sem_cs, sem_cr, True)
 
     block = lax.broadcasted_iota(jnp.int32, (128, CH), 0)
     feature = lax.broadcasted_iota(jnp.int32, (128, CH), 1)
-    spread[...] = jnp.where(block % 32 == feature // 128, 1.0, 0.0).astype(BF16)
+    spread[...] = jnp.where((block & 31) == (feature >> 7), 1.0, 0.0).astype(BF16)
     pay[...] = jnp.zeros(pay.shape, F32)
     bpad[...] = jnp.zeros(bpad.shape, F32)
     bef_all[...] = jnp.zeros(bef_all.shape, F32)
-
-    def wts_on(n):
-        s = 2 * n + z % 2
-        return s, pltpu.make_async_remote_copy(
-            src_ref=wts_r.at[s], dst_ref=wts_r.at[s], send_sem=sem_fw.at[n],
-            recv_sem=sem_wts.at[s], device_id=(me, mate), device_id_type=MESH,
-        )
-
-    def pass_on(n, _):
-        s, copy = wts_on(n)
-        held(wts_r.at[s], sem_wts.at[s])
-        copy.start()
-        return 0
-
-    lax.fori_loop(0, NSEC // 2, pass_on, 0)
 
     for h in range(2):
         held(hid_r.at[h], sem_hr.at[h])
@@ -368,12 +370,6 @@
 
     lax.fori_loop(0, NSEC, weights, 0)
 
-    for h in range(2):
-        held(cot_r.at[h], sem_cr.at[h])
-    cot = join_parts(cot_r)
-    g_ref[...] = cot
-    cw_s[...] = dot(cot.astype(BF16), wu_all[...], NT)
-
     def cw_copy(j):
         return pltpu.make_async_remote_copy(
             src_ref=cw_s.at[pl.ds(pl.multiple_of(8 * peer_chunks[j], 8), 8)],
@@ -382,13 +378,15 @@
             device_id=(peer_segs[j], dp), device_id_type=MESH,
         )
 
-    for j in range(1, NCH):
-        cw_copy(j).start()
-
-    products = dot(wdc_all[...].reshape(256, CH), wuc_all[...], NT)
-    row_sec = lax.broadcasted_iota(jnp.int32, (256, 256), 0) // UNITS
-    col_sec = lanes((256, 256)) // UNITS
-    gram_s[...] = jnp.where(col_sec < row_sec, products, 0.0)
+    def cotangent_products():
+        for h in range(2):
+            held(cot_r.at[h], sem_cr.at[h])
+        cot = join_parts(cot_r)
+        g_ref[...] = cot
+        cw_s[...] = dot(cot.astype(BF16), wu_all[...], NT)
+        for j in range(1, NCH):
+            cw_copy(j).start()
+
     own_gram = pl.ds(pl.multiple_of(32 * chunk, 32), 32)
 
     def gram_copy(j):
@@ -406,8 +404,13 @@
             device_id=(peer_segs[j], dp), device_id_type=MESH,
         )
 
-    for j in range(1, NCH):
-        gram_copy(j).start()
+    def gram_products():
+        products = dot(wdc_all[...].reshape(256, CH), wuc_all[...], NT)
+        row_sec = lax.broadcasted_iota(jnp.int32, (256, 256), 0) >> 4
+        col_sec = lanes((256, 256)) >> 4
+        gram_s[...] = jnp.where(col_sec < row_sec, products, 0.0)
+        for j in range(1, NCH):
+            gram_copy(j).start()
 
     prefetch(0)
     for h in range(2):
@@ -424,7 +427,15 @@
         def _():
             prefetch(s + 2)
 
+        @pl.when(s == 1)
+        def _():
+            cotangent_products()
+
         @pl.when(s == 3)
+        def _():
+            gram_products()
+
+        @pl.when(s == 6)
         def _():
             held(gram_r, sem_gr_r.at[0])
             total = gram_s[own_gram, :]
@@ -525,7 +536,7 @@
         to = 2 * i + h
         ahead = lax.rem(to - z + NZ, NZ)
         return to, pltpu.make_async_remote_copy(
-            src_ref=z_s.at[i, :, 512 * h : 512 * h + 640], dst_ref=z_r.at[ahead],
+            src_ref=z_s.at[i, :, SPLIT[h]], dst_ref=z_r.at[ahead, :, 0 : SIZES[h]],
             send_sem=sem_zs.at[to], recv_sem=sem_zr.at[0],
             device_id=(me, 2 * to + xl), device_id_type=MESH,
         )
@@ -548,28 +559,42 @@
 
     lax.fori_loop(0, NCH, z_send, 0)
     half = z % 2
-    f_total = z_s[z // 2, :, pl.ds(pl.multiple_of(512 * half, 128), 640)].astype(F32)
-    held(z_r.at[1:NZ], sem_zr.at[0])
+    f_total = jnp.concatenate(
+        [z_s[z // 2, :, pl.ds(pl.multiple_of(640 * half, 128), 512)], z_s[z // 2, :, 512:640]],
+        axis=1,
+    ).astype(F32)
+    for h in range(2):
+
+        @pl.when(half == h)
+        def _():
+            held(z_r.at[1:NZ, :, 0 : SIZES[h]], sem_zr.at[0])
+
     f_s[...] = lax.fori_loop(
         1, NZ, lambda n, total: total + z_r[n].astype(F32), f_total
     ).astype(BF16)
 
-    def a_copy(to):
-        return pltpu.make_async_remote_copy(
-            src_ref=f_s, dst_ref=a_r.at[chunk, half], send_sem=sem_as.at[to],
-            recv_sem=sem_ar.at[chunk, half], device_id=(goal, 2 * to + xl), device_id_type=MESH,
+    def a_copy(to, h):
+        return pltpu.make_async_remote_copy(
+            src_ref=f_s.at[:, 0 : SIZES[h]], dst_ref=a_r.at[chunk, h, :, 0 : SIZES[h]],
+            send_sem=sem_as.at[to], recv_sem=sem_ar.at[chunk, h],
+            device_id=(goal, 2 * to + xl), device_id_type=MESH,
         )
 
     def a_send(j, _):
         to = lax.rem(z + j, NZ)
-
-        @pl.when((goal != me) | (to != z))
-        def _():
-            a_copy(to).start()
-
-        @pl.when((goal == me) & (to == z))
-        def _():
-            pltpu.make_async_copy(f_s, a_r.at[chunk, half], sem_ar.at[chunk, half]).start()
+        here = (goal == me) & (to == z)
+        for h in range(2):
+
+            @pl.when(jnp.logical_not(here) & (half == h))
+            def _():
+                a_copy(to, h).start()
+
+            @pl.when(here & (half == h))
+            def _():
+                pltpu.make_async_copy(
+                    f_s.at[:, 0 : SIZES[h]], a_r.at[chunk, h, :, 0 : SIZES[h]],
+                    sem_ar.at[chunk, h],
+                ).start()
 
         return 0
 
@@ -577,13 +602,14 @@
 
     def b_copy(q, h):
         return pltpu.make_async_remote_copy(
-            src_ref=a_r.at[q, h], dst_ref=b_r.at[q, h], send_sem=sem_bs.at[q, h],
+            src_ref=a_r.at[q, h, :, 0 : SIZES[h]], dst_ref=b_r.at[q, h, :, 0 : SIZES[h]],
+            send_sem=sem_bs.at[q, h],
             recv_sem=sem_br.at[q, h], device_id=(me, 2 * z + 1 - xl), device_id_type=MESH,
         )
 
     for q in range(NCH):
         for h in range(2):
-            held(a_r.at[q, h], sem_ar.at[q, h])
+            held(a_r.at[q, h, :, 0 : SIZES[h]], sem_ar.at[q, h])
             b_copy(q, h).start()
 
     for x_to in range(2):
@@ -598,7 +624,7 @@
     held(base_r.at[0 : NSEC - 1], sem_ds.at[2])
 
     def forwarded(n, _):
-        wts_on(n)[1].wait_send()
+        held(wts_r.at[0], sem_fw.at[n])
         return 0
 
     lax.fori_loop(0, NSEC // 2, forwarded, 0)
@@ -635,9 +661,11 @@
     lax.fori_loop(0, NCH, z_left, 0)
 
     def a_left(to, _):
-        @pl.when((goal != me) | (to != z))
-        def _():
-            a_copy(to).wait_send()
+        for h in range(2):
+
+            @pl.when(((goal != me) | (to != z)) & (half == h))
+            def _():
+                a_copy(to, h).wait_send()
 
         return 0
 
@@ -646,9 +674,8 @@
     for q in range(NCH):
         for h in range(2):
             b_copy(q, h).wait_recv()
-            low, cols = (0, slice(CH * q, CH * q + 640)) if h == 0 else (
-                128, slice(CH * q + 640, CH * q + CH))
-            own, other = a_r[q, h][:, low:], b_r[q, h][:, low:]
+            cols = slice(CH * q + SPLIT[h].start, CH * q + SPLIT[h].stop)
+            own, other = a_r[q, h, :, 0 : SIZES[h]], b_r[q, h, :, 0 : SIZES[h]]
             down = jnp.where(xl == 0, own, other)
             up_ref[:, cols] = jnp.where(xl == 0, other, own)
             down_ref[:, cols] = (down.astype(F32) * gains_ref[:, cols].astype(F32)).astype(BF16)

time: 200 us -> 190 us (0.950)
  Pallas kernels: 195 us -> 186 us
    pallas_call x1, Pallas kernels: 195 us -> 186 us  [whole_call(): pl.pallas_call(kernel, name='sections', out_shape=(out, out), in_specs=[p...]
where the time goes in v4:
time: 190 us
  Pallas kernels  186 us (98%)
  local copies, waits for them, and re-layouts  3.39 us (2%)
    pallas_call x1, Pallas kernels, whole_call(): pl.pallas_call(kernel, name='sections', out_shape=(out, out), in_specs=[p...  186 us

profile of v4, /device:TPU:1, one launch (start us, length us, event | category | flops | bytes accessed | tf_op | source)
XLA Modules:
  0.0 189.6 jit_solution(4840798630368976328)
XLA Ops:
  0.6 185.6 %sections.1 = (bf16[16,9216]{1,0:T(8,128)(2,1)}, bf16[16,9216]{1,0:T(8,128)(2,1)}) custom-call(s32[1,8]{1,0:T(1,128)} %ids_ref.1, bf16[8,16,576]{2,1,0:T(8,128)(2,1)} %hid_ref.1, bf16[8,16,576]{2,1,0:T(8,128)(2,1)} %cot_ref.1, bf16[8,16,9216]{2,1,0:T(8,128)(2,1)} %bitcast.10, s32[8,16,72]{2,1,0:T(8,128)} %bitcast.15, bf16[1,9216]{1,0:T(2,128)(2,1)} %gains_ref.1, ...), custom_call_target="tpu_custom_call" | custom-call | tf_op jit(solution)/shard_map/sections/pallas_call | solution.py:699
  186.2 1.7 copy.12
  187.9 1.7 copy.13

commit v5 on v4

--- a/solution.py
+++ b/solution.py
@@ -93,7 +93,8 @@
 
     peer_chunks = [2 * lax.rem(y + dy, 4) + lax.rem(core + dc, 2) for dy, dc in PEERS]
     peer_segs = [seg_of(q) for q in peer_chunks]
-    goal = seg_of(z // 2)
+    pick, half = lax.rem(z % NCH + 4 * core, NCH), z // NCH
+    goal = seg_of(pick)
     mates = [2 * lax.rem(z + step, NZ) + xl for step in (NZ - 1, 1)]
 
     barrier = pltpu.get_barrier_semaphore()
@@ -119,7 +120,7 @@
         def _():
             greet((goal, 2 * j + xl))
 
-        source, at = seg_of(j // 2), 2 * chunk + j % 2
+        source, at = seg_of(j // 2), lax.rem(chunk + 4 * ((j // 2) % 2), NCH) + NCH * (j % 2)
 
         @pl.when((source != me) | (at != z))
         def _():
@@ -241,8 +242,6 @@
     data_send(1)
     data_send(2)
     lax.fori_loop(0, NSEC // 2, pass_on, 0)
-    for x_to in range(2):
-        part_copy(x_to, cot_s, cot_r, sem_cs, sem_cr, True)
 
     block = lax.broadcasted_iota(jnp.int32, (128, CH), 0)
     feature = lax.broadcasted_iota(jnp.int32, (128, CH), 1)
@@ -427,7 +426,12 @@
         def _():
             prefetch(s + 2)
 
-        @pl.when(s == 1)
+        @pl.when(s == 0)
+        def _():
+            for x_to in range(2):
+                part_copy(x_to, cot_s, cot_r, sem_cs, sem_cr, True)
+
+        @pl.when(s == 2)
         def _():
             cotangent_products()
 
@@ -533,7 +537,7 @@
     lax.fori_loop(0, NSEC, grads, 0)
 
     def z_copy(i, h):
-        to = 2 * i + h
+        to = lax.rem(i + 4 * core, NCH) + NCH * h
         ahead = lax.rem(to - z + NZ, NZ)
         return to, pltpu.make_async_remote_copy(
             src_ref=z_s.at[i, :, SPLIT[h]], dst_ref=z_r.at[ahead, :, 0 : SIZES[h]],
@@ -558,9 +562,8 @@
         return 0
 
     lax.fori_loop(0, NCH, z_send, 0)
-    half = z % 2
     f_total = jnp.concatenate(
-        [z_s[z // 2, :, pl.ds(pl.multiple_of(640 * half, 128), 512)], z_s[z // 2, :, 512:640]],
+        [z_s[pick, :, pl.ds(pl.multiple_of(640 * half, 128), 512)], z_s[pick, :, 512:640]],
         axis=1,
     ).astype(F32)
     for h in range(2):
@@ -581,7 +584,8 @@
         )
 
     def a_send(j, _):
-        to = lax.rem(z + j, NZ)
+        ahead = jnp.where(j % 2 == 1, (j + 1) // 2, NZ - j // 2)
+        to = lax.rem(z + ahead, NZ)
         here = (goal == me) & (to == z)
         for h in range(2):
 
@@ -598,7 +602,7 @@
 
         return 0
 
-    lax.fori_loop(0, NZ, a_send, 0)
+    lax.fori_loop(0, NZ, lambda n, _: a_send(NZ - 1 - n, 0), 0)
 
     def b_copy(q, h):
         return pltpu.make_async_remote_copy(

time: 190 us -> 186 us (0.979)
  Pallas kernels: 186 us -> 181 us
    pallas_call x1, Pallas kernels: 186 us -> 181 us  [whole_call(): pl.pallas_call(kernel, name='sections', out_shape=(out, out), in_specs=[p...]
where the time goes in v5:
time: 186 us; the launch traced here: 185 us
  Pallas kernels  181 us (97%)
  local copies, waits for them, and re-layouts  3.39 us (2%)
    pallas_call x1, Pallas kernels, whole_call(): pl.pallas_call(kernel, name='sections', out_shape=(out, out), in_specs=[p...  181 us

profile of v5, /device:TPU:1, one launch (start us, length us, event | category | flops | bytes accessed | tf_op | source)
XLA Modules:
  0.0 185.4 jit_solution(12073908667961548356)
XLA Ops:
  0.6 181.4 %sections.1 = (bf16[16,9216]{1,0:T(8,128)(2,1)}, bf16[16,9216]{1,0:T(8,128)(2,1)}) custom-call(s32[1,8]{1,0:T(1,128)} %ids_ref.1, bf16[8,16,576]{2,1,0:T(8,128)(2,1)} %hid_ref.1, bf16[8,16,576]{2,1,0:T(8,128)(2,1)} %cot_ref.1, bf16[8,16,9216]{2,1,0:T(8,128)(2,1)} %bitcast.10, s32[8,16,72]{2,1,0:T(8,128)} %bitcast.15, bf16[1,9216]{1,0:T(2,128)(2,1)} %gains_ref.1, ...), custom_call_target="tpu_custom_call" | custom-call | tf_op jit(solution)/shard_map/sections/pallas_call | solution.py:703
  182.0 1.7 copy.12
  183.7 1.7 copy.13

commit v6 on v5

--- a/solution.py
+++ b/solution.py
@@ -367,7 +367,9 @@
         ).astype(BF16)
         return 0
 
-    lax.fori_loop(0, NSEC, weights, 0)
+    wuc_all[...] = jnp.zeros(wuc_all.shape, BF16)
+    for s in range(2):
+        weights(s, 0)
 
     def cw_copy(j):
         return pltpu.make_async_remote_copy(
@@ -421,6 +423,12 @@
             finish(s, h)
             start(s + 1, h)
         side_work(s)
+        for k in range(3):
+            later = 2 + 3 * s + k
+
+            @pl.when(later < NSEC)
+            def _():
+                weights(later, 0)
 
         @pl.when(s + 2 < NSEC)
         def _():
@@ -431,15 +439,15 @@
             for x_to in range(2):
                 part_copy(x_to, cot_s, cot_r, sem_cs, sem_cr, True)
 
-        @pl.when(s == 2)
+        @pl.when(s == 5)
         def _():
             cotangent_products()
 
-        @pl.when(s == 3)
+        @pl.when(s == 6)
         def _():
             gram_products()
 
-        @pl.when(s == 6)
+        @pl.when(s == 9)
         def _():
             held(gram_r, sem_gr_r.at[0])
             total = gram_s[own_gram, :]

time: 186 us -> 185 us (level)
  Pallas kernels: 181 us -> 179 us
    pallas_call x1, Pallas kernels: 181 us -> 179 us  [whole_call(): pl.pallas_call(kernel, name='sections', out_shape=(out, out), in_specs=[p...]
where the time goes in v6:
time: 185 us; the launch traced here: 183 us
  Pallas kernels  179 us (97%)
  local copies, waits for them, and re-layouts  3.39 us (2%)
    pallas_call x1, Pallas kernels, whole_call(): pl.pallas_call(kernel, name='sections', out_shape=(out, out), in_specs=[p...  179 us

profile of v6, /device:TPU:1, one launch (start us, length us, event | category | flops | bytes accessed | tf_op | source)
XLA Modules:
  0.0 182.6 jit_solution(11841567745439008721)
XLA Ops:
  0.6 178.5 %sections.1 = (bf16[16,9216]{1,0:T(8,128)(2,1)}, bf16[16,9216]{1,0:T(8,128)(2,1)}) custom-call(s32[1,8]{1,0:T(1,128)} %ids_ref.1, bf16[8,16,576]{2,1,0:T(8,128)(2,1)} %hid_ref.1, bf16[8,16,576]{2,1,0:T(8,128)(2,1)} %cot_ref.1, bf16[8,16,9216]{2,1,0:T(8,128)(2,1)} %bitcast.10, s32[8,16,72]{2,1,0:T(8,128)} %bitcast.15, bf16[1,9216]{1,0:T(2,128)(2,1)} %gains_ref.1, ...), custom_call_target="tpu_custom_call" | custom-call | tf_op jit(solution)/shard_map/sections/pallas_call | solution.py:711
  179.2 1.7 copy.12
  180.9 1.7 copy.13
